TPU v7x, 256 devices: a whole 4x4x8 slice. The times are simulated.
256 devices in a mesh: lev: 8 (over y, core), gx: 4 (over z_hi), gy: 8 (over z_lo, x).
Axes of the slice: x: 4, y: 4, z: 8 (z_hi: 4, z_lo: 2; z = z_hi * 2 + z_lo), core: 2. Of those that a mesh axis runs over, the one named last changes fastest.
Arguments:
- ensemble: float32 [96, 64, 16, 1024], P(None, 'lev', 'gx', 'gy'), may hold values from -6 to 6
- level_scale: float32 [64], P('lev'), may hold values from 0.3 to 1.5
- channel_weights: float32 [4, 64], P(None, 'lev'), may hold values from 0.2 to 1
- error_var: float32 [4], replicated, may hold values from 0.5 to 4
- observed: float32 [2, 4, 512], replicated, may hold values from -8 to 8
- column_x: int32 [2, 512], replicated, may hold values from 0 to 3
- column_y: int32 [2, 512], replicated, may hold values from 0 to 127
- peak_level: int32 [2, 512], replicated, may hold values from 0 to 63
- owner_map: int32 [2], replicated, may hold values from 0 to 31
- courant_x: float32 [64, 16, 1024], P('lev', 'gx', 'gy'), may hold values from -0.3 to 0.3
- courant_y: float32 [64, 16, 1024], P('lev', 'gx', 'gy'), may hold values from -0.3 to 0.3
Outputs:
- analysis: float32 [96, 64, 16, 1024], P(None, 'lev', 'gx', 'gy')
Inputs may be any that keep to these rules, and one draw needn't show every extreme that they name: `owner_map`: block o of columns holds first-dimension columns (o // 8) * 4 onward and second-dimension columns (o % 8) * 128 onward.
All inputs are finite; a program needn't handle non-finite values.
Results may differ from a plain program's by a relative error of at most 0.008.
The roundings to bfloat16 on the way count: a program that leaves them out, or rounds other values in their place, can miss the bound.
Values may be sent and summed in bfloat16 or wider, within the bound.
A program may use at most 64 MiB of HBM per device.

v0:
```python
import math

import jax
import jax.numpy as jnp
from jax import lax
from jax.sharding import PartitionSpec as P

NB = 512
NCH = 4
NBLK = 2
PEAKW = 32
VLOC = 16
HLOC_X = 8
HLOC_Y = 512


KAPPA = 0.1
HIGHEST = lax.Precision.HIGHEST


def from_root(shard, axis, root):
    mine = lax.axis_index(axis) == root
    return lax.psum(jnp.where(mine, shard, jnp.zeros_like(shard)), axis)


def padded_2(cells, sides, width):
    for axis, dim in sides:
        count = lax.axis_size(axis)
        head = lax.slice_in_dim(cells, 0, width, axis=dim)
        tail = lax.slice_in_dim(cells, cells.shape[dim] - width, cells.shape[dim], axis=dim)
        cells = jnp.concatenate(
            [
                lax.ppermute(tail, axis, [(i, (i + 1) % count) for i in range(count)]),
                cells,
                lax.ppermute(head, axis, [((i + 1) % count, i) for i in range(count)]),
            ],
            axis=dim,
        )
    return cells


def periodic_gap(first_pos, second_pos, extent):
    raw_gap = jnp.abs(first_pos - second_pos) % extent
    return jnp.minimum(raw_gap, extent - raw_gap).astype(jnp.float32)


def solve_spd(matrix, right_side):
    factor = jnp.linalg.cholesky(matrix)
    inner_part = lax.linalg.triangular_solve(factor, right_side, left_side=True, lower=True)
    return lax.linalg.triangular_solve(
        factor, inner_part, left_side=True, lower=True, transpose_a=True
    )


def stencil_terms(centre, west, east, south, north, speed_x, speed_y):
    return (
        centre
        - jnp.maximum(speed_x, 0.0) * (centre - west)
        - jnp.minimum(speed_x, 0.0) * (east - centre)
        - jnp.maximum(speed_y, 0.0) * (centre - south)
        - jnp.minimum(speed_y, 0.0) * (north - centre)
        + KAPPA * (east + west + north + south - 4.0 * centre)
    )


def advance(padded, speed_x, speed_y):
    return stencil_terms(
        padded[:, :, 1:-1, 1:-1],
        padded[:, :, :-2, 1:-1],
        padded[:, :, 2:, 1:-1],
        padded[:, :, 1:-1, :-2],
        padded[:, :, 1:-1, 2:],
        speed_x,
        speed_y,
    )


def block_stats(evolved, observed_row, error_inv):
    mean_sim = jnp.mean(evolved, axis=0)
    spread = evolved - mean_sim
    innovation = observed_row - mean_sim
    scaled = spread * error_inv
    cross_term = jnp.dot(scaled, spread.T, precision=HIGHEST)
    pull_vec = jnp.dot(scaled, innovation, precision=HIGHEST)
    return (spread, innovation, scaled, cross_term, pull_vec)


def block_finish(spread, innovation, scaled, cross_term, pull_vec, error_inv):
    members = spread.shape[0]
    system = (members - 1) * jnp.eye(members, dtype=jnp.float32) + cross_term
    combined = solve_spd(system, (pull_vec[None, :] - 0.5 * cross_term).T).T
    increments = error_inv * (innovation - 0.5 * spread) - jnp.dot(
        combined, scaled, precision=HIGHEST
    )
    return (spread.astype(jnp.bfloat16), increments.astype(jnp.bfloat16))


def shards(
    ensemble,
    level_scale,
    channel_weights,
    error_var,
    observed,
    column_x,
    column_y,
    peak_level,
    owner_map,
    courant_x,
    courant_y,
):
    members, levels_here, cells_x, cells_y = ensemble.shape
    row_count = levels_here * cells_x * cells_y
    blocks_x = lax.axis_size("gx")
    blocks_y = lax.axis_size("gy")
    extent_x = cells_x * blocks_x
    extent_y = cells_y * blocks_y
    level_rank = lax.axis_index("lev")
    level_pos = (level_rank * levels_here + jnp.arange(levels_here, dtype=jnp.int32)).astype(
        jnp.float32
    )
    row_x = lax.axis_index("gx") * cells_x + jnp.arange(cells_x, dtype=jnp.int32)
    row_y = lax.axis_index("gy") * cells_y + jnp.arange(cells_y, dtype=jnp.int32)
    error_inv = jnp.repeat(1.0 / error_var, NB)
    current = ensemble
    for block_index in range(NBLK):
        owner_rank = owner_map[block_index]
        local_x = column_x[block_index]
        local_y = column_y[block_index]
        levels = peak_level[block_index]
        flat = current.reshape(members, levels_here, cells_x * cells_y)
        profile = jnp.tanh(
            jnp.take(flat, local_x * cells_y + local_y, axis=2) * level_scale[:, None]
        )
        peak_shape = jnp.exp(
            -jnp.square((level_pos[:, None] - levels[None, :].astype(jnp.float32)) / PEAKW)
        )
        kernel = channel_weights[:, :, None] * peak_shape[None, :, :]
        level_part = jnp.einsum("mlj,klj->mkj", profile, kernel, precision=HIGHEST).reshape(
            members, NCH * NB
        )
        obs_xs = jnp.tile(owner_rank // blocks_y * cells_x + local_x, NCH)
        obs_ys = jnp.tile(owner_rank % blocks_y * cells_y + local_y, NCH)
        obs_level = jnp.tile(levels, NCH).astype(jnp.float32)
        observed_row = observed[block_index].reshape(NCH * NB)
        anomaly = (
            (current - jnp.mean(current, axis=0, keepdims=True))
            .astype(jnp.bfloat16)
            .reshape(members, row_count)
        )
        evolved = lax.psum(level_part, "lev")
        spread, innovation, scaled, cross_term, pull_vec = block_stats(
            evolved, observed_row, error_inv
        )
        block_pert, block_solved = block_finish(
            spread, innovation, scaled, cross_term, pull_vec, error_inv
        )
        block_pert, block_solved = (
            from_root(block_pert, ("gx", "gy"), owner_rank),
            from_root(block_solved, ("gx", "gy"), owner_rank),
        )
        piece_width = block_pert.shape[1]
        sub_width = math.gcd(piece_width, 128)

        def one_sub(running, sub_index):
            offset = sub_index * sub_width
            pert_sub = lax.dynamic_slice_in_dim(block_pert, offset, sub_width, 1)
            solved_sub = lax.dynamic_slice_in_dim(block_solved, offset, sub_width, 1)
            where_x = lax.dynamic_slice_in_dim(obs_xs, 0 + offset, sub_width, 0)
            where_y = lax.dynamic_slice_in_dim(obs_ys, 0 + offset, sub_width, 0)
            where_level = lax.dynamic_slice_in_dim(obs_level, 0 + offset, sub_width, 0)
            taper_v = jnp.exp(-jnp.square((level_pos[:, None] - where_level[None, :]) / VLOC))
            taper_x = jnp.exp(
                -jnp.square(periodic_gap(row_x[:, None], where_x[None, :], extent_x) / HLOC_X)
            )
            taper_y = jnp.exp(
                -jnp.square(periodic_gap(row_y[:, None], where_y[None, :], extent_y) / HLOC_Y)
            )
            taper = (
                taper_v[:, None, None, :] * taper_x[None, :, None, :] * taper_y[None, None, :, :]
            ).reshape(row_count, sub_width)
            covariance = lax.dot_general(
                anomaly, pert_sub, (((0,), (0,)), ((), ())), preferred_element_type=jnp.float32
            )
            weight = (taper * covariance / (members - 1)).astype(jnp.bfloat16)
            update = lax.dot_general(
                solved_sub, weight, (((1,), (1,)), ((), ())), preferred_element_type=jnp.float32
            )
            return (running + update, None)

        start_sum = jnp.zeros((members, row_count), jnp.float32)
        increment = lax.scan(
            one_sub, start_sum, jnp.arange(piece_width // sub_width, dtype=jnp.int32)
        )[0]
        current = current + increment.reshape(current.shape)
    for turn_index in range(2):
        padded = padded_2(current, (("gx", 2), ("gy", 3)), 1)
        current = advance(padded, courant_x, courant_y)
    return current


def solution(mesh):
    in_specs = (
        P(None, "lev", "gx", "gy"),
        P("lev"),
        P(None, "lev"),
        P(),
        P(),
        P(),
        P(),
        P(),
        P(),
        P("lev", "gx", "gy"),
        P("lev", "gx", "gy"),
    )
    out_specs = P(None, "lev", "gx", "gy")
    return jax.shard_map(shards, mesh=mesh, in_specs=in_specs, out_specs=out_specs, check_vma=False)
```

profile of v0, /device:TPU:32, one launch (start us, length us, event | category | flops | bytes accessed | tf_op | source)
XLA Modules:
  0.0 961.5 jit_solution(1714464371236878019)
XLA Ops:
  20.3 5.9 fusion.96
  29.5 68.0 %all-reduce.7.cloned.1.call-done = f32[96,2048]{1,0:T(8,128)} async-done(((f32[96,2048]{1,0:T(8,128)}), f32[96,2048]{1,0:T(8,128)}) %all-reduce.7.cloned.1.call-update) | async-done | bytes 786448 | tf_op jit(solution)/shard_map/psum | solution.py:150
  101.3 8.8 cholesky.44
  111.5 7.4 custom-call.13
  125.8 143.8 %all-reduce.13.cloned.1.call-done = (bf16[96,2048]{1,0:T(8,128)(2,1)}, bf16[96,2048]{1,0:T(8,128)(2,1)}) async-done(((bf16[96,2048]{1,0:T(8,128)(2,1)}, bf16[96,2048]{1,0:T(8,128)(2,1)}), (bf16[96,2048]{1,0:T(8,128)(2,1)}, bf16[96,2048]{1,0:T(8,128)(2,1)})) %all-reduce.13.cloned.1.call-update) | async-done | bytes 786448 | tf_op jit(solution)/shard_map/psum | solution.py:23
  269.6 156.6 %while.28 = (s32[]{:T(128)}, f32[96,4096]{1,0:T(8,128)}, s32[16]{0:T(128)S(1)}, bf16[96,2048]{1,0:T(8,128)(2,1)}, f32[2048]{0:T(1024)S(1)}, /*index=5*/s32[2048]...) while((s32[]{:T(128)}, f32[96,4096]{1,0:T(8,128)}, ...), condition=%wide.region_8.13_spmd.clone, body=%wide.region_7.12_spmd.clone.sunk | while | flops 204539552 | bytes 12561752 | solution.py:191
  295.2 3.3 convolution_add_fusion.4
  305.0 3.3 convolution_add_fusion.4
  314.8 3.3 convolution_add_fusion.4
  324.7 3.3 convolution_add_fusion.4
  334.5 3.3 convolution_add_fusion.4
  344.3 3.3 convolution_add_fusion.4
  364.0 3.3 convolution_add_fusion.4
  373.8 3.3 convolution_add_fusion.4
  383.6 3.3 convolution_add_fusion.4
  413.1 3.3 convolution_add_fusion.4
  423.0 3.3 convolution_add_fusion.4
  426.2 3.3 reshape.427
  434.4 3.9 gather_fusion.1
  438.3 5.9 fusion.99
  448.7 64.3 %all-reduce.9.cloned.1.call-done = f32[96,2048]{1,0:T(8,128)} async-done(((f32[96,2048]{1,0:T(8,128)}), f32[96,2048]{1,0:T(8,128)}) %all-reduce.9.cloned.1.call-update) | async-done | bytes 786448 | tf_op jit(solution)/shard_map/psum | solution.py:150
  516.7 8.8 cholesky.55
  526.8 7.4 custom-call.15
  538.9 146.0 %all-reduce.11.cloned.1.call-done = (bf16[96,2048]{1,0:T(8,128)(2,1)}, bf16[96,2048]{1,0:T(8,128)(2,1)}) async-done(((bf16[96,2048]{1,0:T(8,128)(2,1)}, bf16[96,2048]{1,0:T(8,128)(2,1)}), (bf16[96,2048]{1,0:T(8,128)(2,1)}, bf16[96,2048]{1,0:T(8,128)(2,1)})) %all-reduce.11.cloned.1.call-update) | async-done | bytes 786448 | tf_op jit(solution)/shard_map/psum | solution.py:23
  684.9 157.1 %while.29 = (s32[]{:T(128)}, f32[96,4096]{1,0:T(8,128)}, s32[16]{0:T(128)S(1)}, bf16[96,2048]{1,0:T(8,128)(2,1)}, f32[2048]{0:T(1024)S(1)}, /*index=5*/s32[2048]...) while((s32[]{:T(128)}, f32[96,4096]{1,0:T(8,128)}, ...), condition=%wide.region_15.20_spmd.clone, body=%wide.region_14.19_spmd.clone.sunk | while | flops 204539552 | bytes 12561752 | solution.py:191
  700.6 3.3 convolution_add_fusion.5
  710.5 3.3 convolution_add_fusion.5
  730.2 3.3 convolution_add_fusion.5
  740.1 3.3 convolution_add_fusion.5
  749.9 3.3 convolution_add_fusion.5
  769.7 3.3 convolution_add_fusion.5
  789.4 3.3 convolution_add_fusion.5
  809.1 3.3 convolution_add_fusion.5
  828.9 3.3 convolution_add_fusion.5
  842.0 3.3 reshape.431
  851.4 11.9 %collective-permute-done.1 = f32[96,8,1,128]{3,1,2,0:T(8,128)S(1)} collective-permute-done((f32[96,8,1,128]{3,1,2,0:T(8,128)S(1)}, f32[96,8,1,128]{3,1,2,0:T(8,128)S(1)}, u32[]{:S(2)}, u32[]{:S(2)}) %collective-permute-start.1) | collective-permute-done | bytes 393248 | tf_op jit(solution)/shard_map/ppermute | solution.py:35
  863.4 4.5 collective-permute-done
  869.7 3.8 fusion.172
  882.5 4.6 collective-permute-done.2
  887.0 4.0 copy.95
  891.0 3.9 copy.97
  894.9 8.4 fusion.88
  906.9 13.1 %collective-permute-done.5 = f32[96,8,1,128]{3,1,2,0:T(8,128)S(1)} collective-permute-done((f32[96,8,1,128]{3,1,2,0:T(8,128)S(1)}, f32[96,8,1,128]{3,1,2,0:T(8,128)S(1)}, u32[]{:S(2)}, u32[]{:S(2)}) %collective-permute-start.5) | collective-permute-done | bytes 393248 | tf_op jit(solution)/shard_map/ppermute | solution.py:35
  923.8 3.8 fusion.171
  934.0 4.2 collective-permute-start.7
  938.2 4.0 copy.105
  942.1 3.9 copy.107
  946.0 8.7 fusion.74
  (601 shorter events, 297.2 us)
Async XLA Ops:
  6.5 91.0 %all-reduce.7.cloned.1.call-start = ((), (), s32[]{:S(2)}) async-start(), calls=%async_computation | async-start | bytes 1572864 | tf_op jit(solution)/shard_map/psum | solution.py:150
  17.6 2.7 copy-start.13
  17.6 2.7 copy-start.14
  26.8 1.5 copy-start.15
  26.8 2.3 copy-start
  28.0 1.4 copy-start.10
  28.0 241.6 %all-reduce.13.cloned.1.call-start = ((), (), s32[]{:S(2)}) async-start(), calls=%async_computation.3 | async-start | bytes 1572864 | tf_op jit(solution)/shard_map/psum | solution.py:23
  97.5 21.3 %copy-start.4 = (f32[96,2048]{1,0:T(8,128)S(1)}, f32[96,2048]{1,0:T(8,128)}, u32[]{:S(2)}) copy-start(f32[96,2048]{1,0:T(8,128)} %all-reduce.7.cloned.1.call-done) | copy-start | bytes 2359300
  122.6 390.4 %all-reduce.9.cloned.1.call-start = ((), (), s32[]{:S(2)}) async-start(), calls=%async_computation.1 | async-start | bytes 1572864 | tf_op jit(solution)/shard_map/psum | solution.py:150
  426.2 3.3 copy-start.1
  431.8 106.2 %copy-start.2 = (f32[96,8,4,128]{3,2,1,0:T(4,128)}, f32[96,8,4,128]{3,2,1,0:T(4,128)S(1)}, u32[]{:S(2)}) copy-start(f32[96,8,4,128]{3,2,1,0:T(4,128)S(1)} %get-tuple-element.530) | copy-start | bytes 4718596
  447.8 237.1 %all-reduce.11.cloned.1.call-start = ((), (), s32[]{:S(2)}) async-start(), calls=%async_computation.2 | async-start | bytes 1572864 | tf_op jit(solution)/shard_map/psum | solution.py:23
  513.0 21.1 %copy-start.5 = (f32[96,2048]{1,0:T(8,128)S(1)}, f32[96,2048]{1,0:T(8,128)}, u32[]{:S(2)}) copy-start(f32[96,2048]{1,0:T(8,128)} %all-reduce.9.cloned.1.call-done) | copy-start | bytes 2359300
  842.0 3.3 copy-start.3
  848.0 15.4 %collective-permute-start.1 = (f32[96,8,1,128]{3,1,2,0:T(8,128)S(1)}, f32[96,8,1,128]{3,1,2,0:T(8,128)S(1)}, u32[]{:S(2)}, u32[]{:S(2)}) collective-permute-start(f32[96,8,1,128]{3,1,2,0:T(8,128)S(1)} %bitcast.173), channel_id=1, source_target_pairs={{8,0},{16,8},{24,16},{0,24},{9,1},{17,9},{25,17},{1,25},{10,2},{18... | collective-permute-start | bytes 1179656 | tf_op jit(solution)/shard_map/ppermute | solution.py:35
  851.2 16.7 %collective-permute-start = (f32[96,8,1,128]{3,1,2,0:T(8,128)S(1)}, f32[96,8,1,128]{3,1,2,0:T(8,128)S(1)}, u32[]{:S(2)}, u32[]{:S(2)}) collective-permute-start(f32[96,8,1,128]{3,1,2,0:T(8,128)S(1)} %bitcast.171), channel_id=1, source_target_pairs={{0,8},{8,16},{16,24},{24,0},{1,9},{9,17},{17,25},{25,1},{2,10},{10... | collective-permute-start | bytes 1179656 | tf_op jit(solution)/shard_map/ppermute | solution.py:33
  867.9 0.7 copy-start.6
  876.5 5.3 copy-start.11
  876.5 5.3 copy-start.12
  879.6 11.4 %collective-permute-start.3 = (f32[96,8,6,1]{0,1,3,2:T(8,128)S(1)}, f32[96,8,6,1]{0,1,3,2:T(8,128)S(1)}, u32[]{:S(2)}, u32[]{:S(2)}) collective-permute-start(f32[96,8,6,1]{0,1,3,2:T(8,128)S(1)} %copy.96), channel_id=1, source_target_pairs={{1,0},{2,1},{3,2},{4,3},{5,4},{6,5},{7,6},{0,7},{9,8},{10,9},{11,1... | collective-permute-start | bytes 55304 | tf_op jit(solution)/shard_map/ppermute | solution.py:35
  880.9 6.1 collective-permute-start.2
  903.9 16.1 %collective-permute-start.5 = (f32[96,8,1,128]{3,1,2,0:T(8,128)S(1)}, f32[96,8,1,128]{3,1,2,0:T(8,128)S(1)}, u32[]{:S(2)}, u32[]{:S(2)}) collective-permute-start(f32[96,8,1,128]{3,1,2,0:T(8,128)S(1)} %bitcast.174), channel_id=1, source_target_pairs={{8,0},{16,8},{24,16},{0,24},{9,1},{17,9},{25,17},{1,25},{10,2},{18... | collective-permute-start | bytes 1179656 | tf_op jit(solution)/shard_map/ppermute | solution.py:35
  904.6 18.2 %collective-permute-start.4 = (f32[96,8,1,128]{3,1,2,0:T(8,128)S(1)}, f32[96,8,1,128]{3,1,2,0:T(8,128)S(1)}, u32[]{:S(2)}, u32[]{:S(2)}) collective-permute-start(f32[96,8,1,128]{3,1,2,0:T(8,128)S(1)} %bitcast.172), channel_id=1, source_target_pairs={{0,8},{8,16},{16,24},{24,0},{1,9},{9,17},{17,25},{25,1},{2,10},{10... | collective-permute-start | bytes 1179656 | tf_op jit(solution)/shard_map/ppermute | solution.py:33
  930.7 7.5 collective-permute-start.6
  934.0 8.1 collective-permute-start.7
  942.1 3.9 copy-start.7
  942.1 3.9 copy-start.8
  942.1 3.9 copy-start.9
Sparse Core Ops, SparseCore 0:
  28.1 69.3 all-reduce.6
  122.7 146.8 all-reduce.12
  447.9 65.0 all-reduce.8
  538.0 146.8 all-reduce.10
where the time goes:
time: 968 us; the launch traced here: 962 us
  waiting for transfers between devices  459 us (47%)
  local copies, waits for them, and re-layouts  164 us (17%)
  other arithmetic  155 us (16%)
  matrix products  125 us (13%)
  loops' own time  23.2 us (2%)
  between operations  20.5 us (2%)
  starting transfers between devices  13.9 us (1%)
    psum x2, waiting for transfers between devices, from_root(): return lax.psum(jnp.where(mine, shard, jnp.zeros_like(shard)), axis)  290 us
    psum x2, waiting for transfers between devices, shards(): evolved = lax.psum(level_part, 'lev')  132 us
    dot_general x32, matrix products, one_sub(): lax.dot_general(solved_sub, weight, (((1,), (1,)), ((), ())), preferred_e...  103 us
    mul x64, other arithmetic, one_sub(): taper_v[:, None, None, :] * taper_x[None, :, None, :]  77.6 us
    mul x32, local copies, waits for them, and re-layouts, one_sub(): taper_v[:, None, None, :] * taper_x[None, :, None, :]  67.3 us
    ppermute x4, waiting for transfers between devices, padded_2(): lax.ppermute(head, axis, [((i + 1) % count, i) for i in range(count)])  25 us
    another operation x2, loops' own time, shards(): lax.scan(one_sub, start_sum, jnp.arange(piece_width // sub_width, dtype=j...  23.2 us
    dynamic_slice x32, local copies, waits for them, and re-layouts, shards(): lax.scan(one_sub, start_sum, jnp.arange(piece_width // sub_width, dtype=j...  20.9 us
  transfers between devices with their start and end apart: 12, of which 9 were waited for; matrix products, arithmetic and copies ran while one was open for 2% of the time, Pallas kernels for 0%

commit v1 on v0

v1 whole, which is shorter than its diff:
```python
import jax
import jax.numpy as jnp
from jax import lax
from jax.experimental import pallas as pl
from jax.experimental.pallas import tpu as pltpu
from jax.sharding import PartitionSpec as P

NB = 512
NCH = 4
NBLK = 2
PEAKW = 32
VLOC = 16
HLOC_X = 8
HLOC_Y = 512
KAPPA = 0.1

M = 96
LEV = 8
CX = 4
CY = 128
COLS = CX * CY
ROWS = LEV * CX
HALF = 256
PIECE = 24

F32 = jnp.float32
BF16 = jnp.bfloat16
HIGHEST = lax.Precision.HIGHEST
MESH = pl.DeviceIdType.MESH
VMEM_LIMIT = 56 * 1024 * 1024


def split3(value):
    high = value.astype(BF16)
    rest = value - high.astype(F32)
    middle = rest.astype(BF16)
    low = (rest - middle.astype(F32)).astype(BF16)
    return high, middle, low


def partial_kernel(scale_ref, weight_ref, state_ref, column_ref, peak_ref, out_ref, gathered):
    first_level = (lax.axis_index("lev") * LEV).astype(F32)
    chosen = (lax.broadcasted_iota(jnp.int32, (COLS, NB), 0) == column_ref[...]).astype(F32)
    chosen = chosen.astype(BF16)
    for level in range(LEV):
        profile = jnp.concatenate(
            [jnp.tanh(state_ref[level * CX + x] * scale_ref[level]) for x in range(CX)], axis=1
        )
        parts = jnp.concatenate(split3(profile), axis=0)
        picked = jnp.dot(parts, chosen, preferred_element_type=F32)
        gathered[level] = picked[:M] + picked[M : 2 * M] + picked[2 * M :]
    peak = peak_ref[...].astype(F32)
    shapes = [
        jnp.exp(-jnp.square((first_level + level - peak) / PEAKW)) for level in range(LEV)
    ]
    for tile in range(4):
        lanes = slice(tile * 128, tile * 128 + 128)
        for channel in range(NCH):
            total = jnp.zeros((M, 128), F32)
            for level in range(LEV):
                total += gathered[level, :, lanes] * (
                    shapes[level][:, lanes] * weight_ref[channel, level]
                )
            half, quarter = tile // 2, tile % 2
            out_ref[half, channel, quarter * M : quarter * M + M, :] = total


def device_at(x, z, lev):
    return (lev, lax.div(z, 2), lax.rem(z, 2) * 4 + x)


def share_kernel(
    owner_ref, part_ref, out_ref, from_core, sums, from_y, from_z, from_x, send, recv
):
    lev = lax.axis_index("lev")
    gx = lax.axis_index("gx")
    gy = lax.axis_index("gy")
    core, y = lax.rem(lev, 2), lax.div(lev, 2)
    x, z = lax.rem(gy, 4), gx * 2 + lax.div(gy, 4)
    other = y * 2 + 1 - core
    owner = owner_ref[0]
    owner_z = lax.div(owner, 8) * 2 + lax.div(lax.rem(owner, 8), 4)
    owner_x = lax.rem(owner, 4)

    y_at = lambda d: lax.rem(y + d, 4)
    z_at = lambda d: lax.rem(z + d, 8)
    x_at = lambda d: lax.rem(x + d, 4)
    to_core = device_at(x, z, other)
    to_y = lambda d: device_at(x, z, y_at(d) * 2 + core)
    to_z = lambda d: device_at(x, z_at(d), lev)
    to_x = lambda d: device_at(x_at(d), z, lev)

    barrier = pltpu.get_barrier_semaphore()
    peers = [to_core] + [to_y(d) for d in range(1, 4)]
    peers += [to_z(d) for d in range(1, 8)] + [to_x(d) for d in range(1, 4)]
    for peer in peers:
        pl.semaphore_signal(barrier, inc=1, device_id=peer, device_id_type=MESH)
    pl.semaphore_wait(barrier, len(peers))

    slot = [0]

    def start(src, dst, device):
        number = slot[0]
        slot[0] += 1
        copy = pltpu.make_async_remote_copy(
            src_ref=src,
            dst_ref=dst,
            send_sem=send.at[number],
            recv_sem=recv.at[number],
            device_id=device,
            device_id_type=MESH,
        )
        copy.start()
        return copy

    started = []
    order = (1, 2, 3, 0)
    core_copies = [
        start(part_ref.at[1 - core, y_at(d)], from_core.at[y_at(d)], to_core) for d in order
    ]
    y_copies = []
    for d, copy in zip(order, core_copies):
        copy.wait_recv()
        where = y_at(d)
        sums[where] = part_ref[core, where] + from_core[where]
        if d > 0:
            y_copies.append(start(sums.at[where], from_y.at[d - 1], to_y(d)))
    started += core_copies + y_copies
    for copy in y_copies:
        copy.wait_recv()
    total = sums[y] + from_y[0] + from_y[1] + from_y[2]
    sums[y] = total

    z_copies = [
        start(sums.at[y, pl.ds(z_at(d) * PIECE, PIECE)], from_z.at[z], to_z(d))
        for d in range(1, 8)
    ]
    from_z[z] = sums[y, pl.ds(pl.multiple_of(z * PIECE, 8), PIECE)]
    for copy in z_copies:
        copy.wait_recv()
    started += z_copies
    from_x[x] = from_z[owner_z]
    x_copies = [start(from_x.at[x], from_x.at[x], to_x(d)) for d in range(1, 4)]
    for copy in x_copies:
        copy.wait_recv()
    started += x_copies

    mine = pl.ds(pl.multiple_of(z * PIECE, 8), PIECE)
    out_ref[core, y, mine] = from_x[owner_x]
    z_copies = [
        start(out_ref.at[core, y, mine], out_ref.at[core, y, mine], to_z(d)) for d in range(1, 8)
    ]
    for copy in z_copies:
        copy.wait_recv()
    started += z_copies
    y_copies = [
        start(out_ref.at[core, y], out_ref.at[core, y], to_y(d)) for d in range(1, 4)
    ]
    core_copies = [start(out_ref.at[core, y], out_ref.at[core, y], to_core)]
    for d, copy in zip(range(1, 4), y_copies):
        copy.wait_recv()
        came = out_ref.at[core, y_at(4 - d)]
        core_copies.append(start(came, came, to_core))
    for copy in core_copies:
        copy.wait_recv()
    started += y_copies + core_copies
    for copy in started:
        copy.wait_send()


N_COPIES = 4 + 3 + 7 + 3 + 7 + 3 + 4


def update_kernel(
    owner_ref,
    inverse_ref,
    state_ref,
    evolved_ref,
    observed_ref,
    column_x_ref,
    column_y_ref,
    peak_ref,
    out_ref,
    spread,
    scaled,
    innovation,
    pert,
    solved_t,
    taper_y,
    taper_vx,
    weight,
):
    owner = owner_ref[0]
    for channel in range(NCH):
        inverse = inverse_ref[channel]
        for tile in range(4):
            half, quarter = tile // 2, tile % 2
            evolved = evolved_ref[half, channel, quarter * M : quarter * M + M, :]
            mean = jnp.sum(evolved, axis=0, keepdims=True) * (1.0 / M)
            lanes = slice(channel * NB + tile * 128, channel * NB + tile * 128 + 128)
            part = evolved - mean
            spread[:, lanes] = part
            pert[:, lanes] = part.astype(BF16)
            scaled[:M, lanes] = part * inverse
            away = observed_ref[channel : channel + 1, tile * 128 : tile * 128 + 128] - mean
            innovation[:, lanes] = away
            scaled[M:, lanes] = jnp.broadcast_to(away * inverse, (8, 128))
    cross = lax.dot_general(
        scaled[...], spread[...], (((1,), (1,)), ((), ())), precision=HIGHEST,
        preferred_element_type=F32,
    )
    lane = lax.broadcasted_iota(jnp.int32, (M + 8, 128), 1)
    row = lax.broadcasted_iota(jnp.int32, (M + 8, 128), 0)
    cross = jnp.concatenate([cross, jnp.zeros((M + 8, 128 - M), F32)], axis=1)
    system = cross + jnp.where((lane == row) & (row < M), float(M - 1), 0.0)

    def sweep(pivot, matrix):
        at_row, at_lane = row == pivot, lane == pivot
        pivot_row = jnp.sum(jnp.where(at_row, matrix, 0.0), axis=0, keepdims=True)
        column = jnp.sum(jnp.where(at_lane, matrix, 0.0), axis=1, keepdims=True)
        first = lane[:1] == pivot
        corner = jnp.sum(jnp.where(first, pivot_row, 0.0), axis=1, keepdims=True)
        scale = 1.0 / corner
        times = jnp.where(first, -1.0, pivot_row) * scale
        column = jnp.where(row[:, :1] == pivot, -1.0, column)
        return jnp.where(at_row | at_lane, 0.0, matrix) - column * times

    swept = lax.fori_loop(0, M, sweep, system)
    gain = (swept[M : M + 1] - 0.5 * (M - 1) * swept[:M])[:, :M]
    for channel in range(NCH):
        lanes = slice(channel * NB, channel * NB + NB)
        change = jnp.dot(gain, spread[:, lanes], precision=HIGHEST, preferred_element_type=F32)
        solved = inverse_ref[channel] * (innovation[:, lanes] - change)
        solved_t[lanes, :] = solved.T.astype(BF16)

    peak = peak_ref[...].astype(F32)
    at_x = lax.div(owner, 8) * CX + column_x_ref[...]
    at_y = lax.rem(owner, 8) * CY + column_y_ref[...]
    grid_y = lax.axis_index("gy") * CY + lax.broadcasted_iota(jnp.int32, (CY, NB), 0)
    gap = jnp.abs(grid_y - at_y)
    gap = jnp.minimum(gap, 8 * CY - gap).astype(F32)
    taper_y[...] = jnp.exp(-jnp.square(gap / HLOC_Y))
    index = lax.broadcasted_iota(jnp.int32, (ROWS, NB), 0)
    grid_x = lax.axis_index("gx") * CX + lax.rem(index, CX)
    gap = jnp.abs(grid_x - at_x)
    gap = jnp.minimum(gap, 4 * CX - gap).astype(F32)
    level = (lax.axis_index("lev") * LEV + lax.div(index, CX)).astype(F32)
    taper_vx[...] = (
        jnp.exp(-jnp.square((level - peak) / VLOC)) * jnp.exp(-jnp.square(gap / HLOC_X))
    ) * (1.0 / (M - 1))

    @pl.loop(0, ROWS)
    def _(at):
        state = state_ref[at]
        anomaly = (state - jnp.sum(state, axis=0, keepdims=True) * (1.0 / M)).T.astype(BF16)
        beside = taper_vx[pl.ds(at, 1), :]
        for chunk in range(NB // HALF):
            near = slice(chunk * HALF, chunk * HALF + HALF)
            taper = taper_y[:, near] * beside[:, near]
            for channel in range(NCH):
                lanes = slice(channel * NB + chunk * HALF, channel * NB + chunk * HALF + HALF)
                covariance = jnp.dot(anomaly, pert[:, lanes], preferred_element_type=F32)
                weight[:, lanes] = (taper * covariance).astype(BF16)
        update = jnp.dot(weight[...], solved_t[...], preferred_element_type=F32)
        out_ref[at] = state + update.T


def stencil_kernel(
    speed_x_ref, speed_y_ref, state_ref, out_ref, middle, face, got, edge, came, send, recv
):
    lev = lax.axis_index("lev")
    gx = lax.axis_index("gx")
    gy = lax.axis_index("gy")
    up_x = (lev, lax.rem(gx + 1, 4), gy)
    down_x = (lev, lax.rem(gx + 3, 4), gy)
    up_y = (lev, gx, lax.rem(gy + 1, 8))
    down_y = (lev, gx, lax.rem(gy + 7, 8))
    targets = (up_x, down_x, up_y, down_y)
    barrier = pltpu.get_barrier_semaphore()
    for peer in targets:
        pl.semaphore_signal(barrier, inc=1, device_id=peer, device_id_type=MESH)
    pl.semaphore_wait(barrier, 4)
    lane = lax.broadcasted_iota(jnp.int32, (M, CY), 1)

    for turn in range(2):
        source = state_ref if turn == 0 else middle
        target = middle if turn == 0 else out_ref

        def start(number, src, dst):
            copy = pltpu.make_async_remote_copy(
                src_ref=src,
                dst_ref=dst,
                send_sem=send.at[turn, number],
                recv_sem=recv.at[turn, number],
                device_id=targets[number],
                device_id_type=MESH,
            )
            copy.start()
            return copy

        def pack(level, carry):
            last, first = carry
            face[turn, 0, level] = source[level * CX + CX - 1].astype(BF16)
            face[turn, 1, level] = source[level * CX].astype(BF16)
            for x in range(CX):
                tile = source[level * CX + x]
                here = lane == level * CX + x
                last = jnp.where(here, tile[:, CY - 1 :], last)
                first = jnp.where(here, tile[:, :1], first)
            return last, first

        nothing = jnp.zeros((M, CY), F32)
        last, first = lax.fori_loop(0, LEV, pack, (nothing, nothing))
        edge[turn, 0] = last
        edge[turn, 1] = first
        copies = [start(n, face.at[turn, n], got.at[turn, n]) for n in range(2)]
        copies += [start(2 + n, edge.at[turn, n], came.at[turn, n]) for n in range(2)]
        for copy in copies:
            copy.wait()

        @pl.loop(0, LEV)
        def _(level):
            shift = lax.rem(CY - level * CX, CY)
            souths = pltpu.roll(came[turn, 0], shift, 1)
            norths = pltpu.roll(came[turn, 1], shift, 1)
            for x in range(CX):
                at = level * CX + x
                centre = source[at]
                west = source[at - 1] if x > 0 else got[turn, 0, level].astype(F32)
                east = source[at + 1] if x < CX - 1 else got[turn, 1, level].astype(F32)
                south = jnp.where(lane == 0, souths[:, x : x + 1], pltpu.roll(centre, 1, 1))
                north = jnp.where(
                    lane == CY - 1, norths[:, x : x + 1], pltpu.roll(centre, CY - 1, 1)
                )
                u = speed_x_ref[pl.ds(at, 1), :]
                v = speed_y_ref[pl.ds(at, 1), :]
                target[at] = (
                    centre * (1.0 - 4.0 * KAPPA - jnp.abs(u) - jnp.abs(v))
                    + west * (jnp.maximum(u, 0.0) + KAPPA)
                    + east * (KAPPA - jnp.minimum(u, 0.0))
                    + south * (jnp.maximum(v, 0.0) + KAPPA)
                    + north * (KAPPA - jnp.minimum(v, 0.0))
                )


SMEM_SPEC = pl.BlockSpec(memory_space=pltpu.SMEM)
VMEM_SPEC = pl.BlockSpec(memory_space=pltpu.VMEM)


def partial(scale, weights, state, column, peak):
    return pl.pallas_call(
        partial_kernel,
        out_shape=jax.ShapeDtypeStruct((2, NCH, 2 * M, 128), F32),
        in_specs=[SMEM_SPEC] * 2 + [VMEM_SPEC] * 3,
        out_specs=VMEM_SPEC,
        scratch_shapes=[pltpu.VMEM((LEV, M, NB), F32)],
        compiler_params=pltpu.CompilerParams(vmem_limit_bytes=VMEM_LIMIT),
        name="partial",
    )(scale, weights, state, column, peak)


def share(number, owner, part):
    return pl.pallas_call(
        share_kernel,
        out_shape=jax.ShapeDtypeStruct((2, NCH, 2 * M, 128), F32),
        in_specs=[SMEM_SPEC, VMEM_SPEC],
        out_specs=VMEM_SPEC,
        scratch_shapes=[
            pltpu.VMEM((4, 2 * M, 128), F32),
            pltpu.VMEM((4, 2 * M, 128), F32),
            pltpu.VMEM((3, 2 * M, 128), F32),
            pltpu.VMEM((8, PIECE, 128), F32),
            pltpu.VMEM((4, PIECE, 128), F32),
            pltpu.SemaphoreType.DMA((N_COPIES,)),
            pltpu.SemaphoreType.DMA((N_COPIES,)),
        ],
        compiler_params=pltpu.CompilerParams(
            vmem_limit_bytes=VMEM_LIMIT, collective_id=number, has_side_effects=True
        ),
        name="share",
    )(owner, part)


def update(owner, inverse, state, evolved, observed, column_x, column_y, peak):
    return pl.pallas_call(
        update_kernel,
        out_shape=jax.ShapeDtypeStruct((ROWS, M, CY), F32),
        in_specs=[SMEM_SPEC] * 2 + [VMEM_SPEC] * 6,
        out_specs=VMEM_SPEC,
        scratch_shapes=[
            pltpu.VMEM((M, NCH * NB), F32),
            pltpu.VMEM((M + 8, NCH * NB), F32),
            pltpu.VMEM((1, NCH * NB), F32),
            pltpu.VMEM((M, NCH * NB), BF16),
            pltpu.VMEM((NCH * NB, M), BF16),
            pltpu.VMEM((CY, NB), F32),
            pltpu.VMEM((ROWS, NB), F32),
            pltpu.VMEM((CY, NCH * NB), BF16),
        ],
        compiler_params=pltpu.CompilerParams(vmem_limit_bytes=VMEM_LIMIT),
        name="update",
    )(owner, inverse, state, evolved, observed, column_x, column_y, peak)


def transport(speed_x, speed_y, state):
    return pl.pallas_call(
        stencil_kernel,
        out_shape=jax.ShapeDtypeStruct((ROWS, M, CY), F32),
        in_specs=[VMEM_SPEC] * 3,
        out_specs=VMEM_SPEC,
        scratch_shapes=[
            pltpu.VMEM((ROWS, M, CY), F32),
            pltpu.VMEM((2, 2, LEV, M, CY), BF16),
            pltpu.VMEM((2, 2, LEV, M, CY), BF16),
            pltpu.VMEM((2, 2, M, CY), F32),
            pltpu.VMEM((2, 2, M, CY), F32),
            pltpu.SemaphoreType.DMA((2, 4)),
            pltpu.SemaphoreType.DMA((2, 4)),
        ],
        compiler_params=pltpu.CompilerParams(
            vmem_limit_bytes=VMEM_LIMIT, collective_id=NBLK, has_side_effects=True
        ),
        name="transport",
    )(speed_x, speed_y, state)


def shards(
    ensemble,
    level_scale,
    channel_weights,
    error_var,
    observed,
    column_x,
    column_y,
    peak_level,
    owner_map,
    courant_x,
    courant_y,
):
    state = ensemble.reshape(M, ROWS, CY).transpose(1, 0, 2)
    inverse = 1.0 / error_var
    columns = column_x * CY + column_y
    for block in range(NBLK):
        one = slice(block, block + 1)
        owner, peak = owner_map[one], peak_level[one]
        part = partial(level_scale, channel_weights, state, columns[one], peak)
        evolved = share(block, owner, part)
        state = update(
            owner, inverse, state, evolved, observed[block], column_x[one], column_y[one], peak
        )
    result = transport(courant_x.reshape(ROWS, CY), courant_y.reshape(ROWS, CY), state)
    return result.transpose(1, 0, 2).reshape(ensemble.shape)


def solution(mesh):
    in_specs = (
        P(None, "lev", "gx", "gy"),
        P("lev"),
        P(None, "lev"),
        P(),
        P(),
        P(),
        P(),
        P(),
        P(),
        P("lev", "gx", "gy"),
        P("lev", "gx", "gy"),
    )
    out_specs = P(None, "lev", "gx", "gy")
    return jax.shard_map(shards, mesh=mesh, in_specs=in_specs, out_specs=out_specs, check_vma=False)
```

time: 968 us -> 208 us (0.21)
  waiting for transfers between devices: 459 us -> 0 us
  Pallas kernels: 0 us -> 192 us
  other arithmetic: 155 us -> 1.89 us
  local copies, waits for them, and re-layouts: 164 us -> 12.4 us
  matrix products: 125 us -> 0 us
  loops' own time: 23.2 us -> 0 us
  between operations: 20.5 us -> 0.03 us
  starting transfers between devices: 13.9 us -> 0 us
    psum x4 -> x0, waiting for transfers between devices: 422 us -> none  [the longest x2 290 us: from_root(): return lax.psum(jnp.where(mine, shard, jnp.zeros_like(shard)), axis)]
    pallas_call x0 -> x7, Pallas kernels: none -> 192 us  [the longest x2 74.2 us: share(): pl.pallas_call(share_kernel, out_shape=jax.ShapeDtypeStruct((2, NCH, 2 *...]
    dot_general x40 -> x0, matrix products: 124 us -> none  [the longest x32 103 us: one_sub(): lax.dot_general(solved_sub, weight, (((1,), (1,)), ((), ())), preferred_e...]
    mul x64 -> x0, other arithmetic: 77.6 us -> none  [one_sub(): taper_v[:, None, None, :] * taper_x[None, :, None, :]]
    mul x32 -> x0, local copies, waits for them, and re-layouts: 67.3 us -> none  [one_sub(): taper_v[:, None, None, :] * taper_x[None, :, None, :]]
    ppermute x8 -> x0, waiting for transfers between devices: 36.9 us -> none  [the longest x4 25 us: padded_2(): lax.ppermute(head, axis, [((i + 1) % count, i) for i in range(count)])]
    another operation x10 -> x0, other arithmetic: 34.9 us -> none  [the longest x6 18.9 us: solve_spd(): factor = jnp.linalg.cholesky(matrix)]
    dynamic_slice x128 -> x0, local copies, waits for them, and re-layouts: 28.2 us -> none  [the longest x32 20.9 us: shards(): lax.scan(one_sub, start_sum, jnp.arange(piece_width // sub_width, dtype=j...]
  transfers between devices with their start and end apart: 12 -> 0, of which waited for: 9 -> 0; matrix products, arithmetic and copies ran while one was open for 2% -> 0% of each run, Pallas kernels for 0% -> 0%
where the time goes in v1:
time: 208 us; the launch traced here: 206 us
  Pallas kernels  192 us (92%)
  local copies, waits for them, and re-layouts  12.4 us (6%)
    pallas_call x2, Pallas kernels, share(): pl.pallas_call(share_kernel, out_shape=jax.ShapeDtypeStruct((2, NCH, 2 *...  74.2 us
    pallas_call x2, Pallas kernels, update(): pl.pallas_call(update_kernel, out_shape=jax.ShapeDtypeStruct((ROWS, M, CY...  73.2 us
    pallas_call x1, Pallas kernels, transport(): pl.pallas_call(stencil_kernel, out_shape=jax.ShapeDtypeStruct((ROWS, M, C...  36.6 us
    pallas_call x2, Pallas kernels, partial(): pl.pallas_call(partial_kernel, out_shape=jax.ShapeDtypeStruct((2, NCH, 2...  7.77 us

profile of v1, /device:TPU:32, one launch (start us, length us, event | category | flops | bytes accessed | tf_op | source)
XLA Modules:
  0.0 206.1 jit_solution(9046710819100368310)
XLA Ops:
  0.0 1.2 broadcast_divide_fusion.inverse_ref
  1.2 1.3 fusion.4
  2.5 0.7 multiply_add_fusion
  3.2 1.4 fusion.2
  4.6 1.4 fusion
  5.9 1.3 slice_bitcast_fusion
  7.3 3.5 %copy.12 = f32[96,8,4,128]{3,0,2,1:T(8,128)} copy(f32[96,8,4,128]{3,2,1,0:T(4,128)} %param.11) | data formatting | bytes 3145728 | tf_op args[0]
  10.7 3.9 %partial.2.part_ref = f32[2,4,192,128]{3,2,1,0:T(8,128)} custom-call(f32[8]{0:T(128)} %scale_ref.3, f32[4,8]{1,0:T(4,128)} %weight_ref.3, f32[32,96,128]{2,1,0:T(8,128)} %bitcast.12, s32[1,512]{1,0:T(1,128)} %get-tuple-element.17.column_ref, s32[1,512]{1,0:T(1,128)} %get-tuple-element.12.peak_ref), custom_call_target="tpu_custom_call" | custom-call | tf_op jit(solution)/shard_map/partial/pallas_call | solution.py:351
  14.6 39.9 %share.2.evolved_ref = f32[2,4,192,128]{3,2,1,0:T(8,128)} custom-call(s32[1]{0:T(128)} %get-tuple-element.15.owner_ref, f32[2,4,192,128]{3,2,1,0:T(8,128)} %partial.2.part_ref), custom_call_target="tpu_custom_call" | custom-call | tf_op jit(solution)/shard_map/share/pallas_call | solution.py:363
  54.6 36.8 %update.2.state_ref = f32[32,96,128]{2,1,0:T(8,128)} custom-call(s32[1]{0:T(128)} %get-tuple-element.15.owner_ref, f32[4]{0:T(128)} %broadcast_divide_fusion.inverse_ref, f32[32,96,128]{2,1,0:T(8,128)} %bitcast.13, f32[2,4,192,128]{3,2,1,0:T(8,128)} %share.2.evolved_ref, f32[4,512]{1,0:T(4,128)} %get-tuple-element.6.observed_ref, ...), custom_call_target="tpu_custom_call" | custom-call | tf_op jit(solution)/shard_map/update/pallas_call | solution.py:385
  91.3 3.9 %partial.3.part_ref = f32[2,4,192,128]{3,2,1,0:T(8,128)} custom-call(f32[8]{0:T(128)} %scale_ref.3, f32[4,8]{1,0:T(4,128)} %weight_ref.3, f32[32,96,128]{2,1,0:T(8,128)} %update.2.state_ref, s32[1,512]{1,0:T(1,128)} %get-tuple-element.18.column_ref, s32[1,512]{1,0:T(1,128)} %get-tuple-element.11.peak_ref), custom_call_target="tpu_custom_call" | custom-call | tf_op jit(solution)/shard_map/partial/pallas_call | solution.py:351
  95.2 34.3 %share.3.evolved_ref = f32[2,4,192,128]{3,2,1,0:T(8,128)} custom-call(s32[1]{0:T(128)} %get-tuple-element.16.owner_ref, f32[2,4,192,128]{3,2,1,0:T(8,128)} %partial.3.part_ref), custom_call_target="tpu_custom_call" | custom-call | tf_op jit(solution)/shard_map/share/pallas_call | solution.py:363
  129.5 36.5 %update.3.state_ref = f32[32,96,128]{2,1,0:T(8,128)} custom-call(s32[1]{0:T(128)} %get-tuple-element.16.owner_ref, f32[4]{0:T(128)} %broadcast_divide_fusion.inverse_ref, f32[32,96,128]{2,1,0:T(8,128)} %update.2.state_ref, f32[2,4,192,128]{3,2,1,0:T(8,128)} %share.3.evolved_ref, f32[4,512]{1,0:T(4,128)} %get-tuple-element.5.observed_ref, ...), custom_call_target="tpu_custom_call" | custom-call | tf_op jit(solution)/shard_map/update/pallas_call | solution.py:385
  166.0 36.6 %transport.1 = f32[32,96,128]{2,1,0:T(8,128)} custom-call(f32[32,128]{1,0:T(8,128)} %bitcast.15, f32[32,128]{1,0:T(8,128)} %bitcast.16, f32[32,96,128]{2,1,0:T(8,128)} %update.3.state_ref), custom_call_target="tpu_custom_call" | custom-call | tf_op jit(solution)/shard_map/transport/pallas_call | solution.py:406
  202.5 3.6 %copy.13 = f32[96,8,4,128]{3,2,1,0:T(4,128)} copy(f32[96,8,4,128]{3,0,2,1:T(8,128)} %bitcast.14) | data formatting | bytes 3145728 | tf_op jit(solution)/shard_map/reshape | solution.py:452

commit v2 on v0

v2 whole, which is shorter than its diff:
```python
import jax
import jax.numpy as jnp
from jax import lax
from jax.experimental import pallas as pl
from jax.experimental.pallas import tpu as pltpu
from jax.sharding import PartitionSpec as P

NB = 512
NCH = 4
NBLK = 2
PEAKW = 32
VLOC = 16
HLOC_X = 8
HLOC_Y = 512
KAPPA = 0.1

M = 96
LEV = 8
CX = 4
CY = 128
COLS = CX * CY
ROWS = LEV * CX
HALF = 256
GROUP = 4
LAST = 8
STEPS = M // ROWS * GROUP
PIECE = 24
SOME = LAST // CX
N_FACES = 2 * (2 * (LEV // SOME) + 2)

F32 = jnp.float32
BF16 = jnp.bfloat16
HIGHEST = lax.Precision.HIGHEST
MESH = pl.DeviceIdType.MESH
VMEM_LIMIT = 56 * 1024 * 1024


def split3(value):
    high = value.astype(BF16)
    rest = value - high.astype(F32)
    middle = rest.astype(BF16)
    low = (rest - middle.astype(F32)).astype(BF16)
    return high, middle, low


def radiances(block, scale_ref, weight_ref, state, column_x_ref, column_y_ref, peak_ref, part, gathered):
    one = slice(block, block + 1)
    column = column_x_ref[one, :] * CY + column_y_ref[one, :]
    first_level = (lax.axis_index("lev") * LEV).astype(F32)
    chosen = (lax.broadcasted_iota(jnp.int32, (COLS, NB), 0) == column).astype(F32)
    chosen = chosen.astype(BF16)
    for level in range(LEV):
        profile = jnp.concatenate(
            [jnp.tanh(state[level * CX + x] * scale_ref[level]) for x in range(CX)], axis=1
        )
        parts = jnp.concatenate(split3(profile), axis=0)
        picked = jnp.dot(parts, chosen, preferred_element_type=F32)
        gathered[level] = picked[:M] + picked[M : 2 * M] + picked[2 * M :]
    peak = peak_ref[one, :].astype(F32)
    shapes = [
        jnp.exp(-jnp.square((first_level + level - peak) / PEAKW)) for level in range(LEV)
    ]

    def produce(channel):
        factors = [shapes[level] * weight_ref[channel, level] for level in range(LEV)]
        for tile in range(4):
            lanes = slice(tile * 128, tile * 128 + 128)
            half, quarter = tile // 2, tile % 2
            total = gathered[0, :, lanes] * factors[0][:, lanes]
            for level in range(1, LEV):
                total += gathered[level, :, lanes] * factors[level][:, lanes]
            part[half, channel, quarter * M : quarter * M + M, :] = total

    return produce


def place():
    lev, gx, gy = lax.axis_index("lev"), lax.axis_index("gx"), lax.axis_index("gy")
    core, y = lax.rem(lev, 2), lax.div(lev, 2)
    x, z = lax.rem(gy, 4), gx * 2 + lax.div(gy, 4)

    def at(dx, dy, dz, dcore):
        there_x, there_y = lax.rem(x + dx, 4), lax.rem(y + dy, 4)
        there_z, there_core = lax.rem(z + dz, 8), lax.rem(core + dcore, 2)
        return (
            there_y * 2 + there_core,
            lax.div(there_z, 2),
            lax.rem(there_z, 2) * 4 + there_x,
        )

    beside = (
        (lev, lax.rem(gx + 1, 4), gy),
        (lev, lax.rem(gx + 3, 4), gy),
        (lev, gx, lax.rem(gy + 1, 8)),
        (lev, gx, lax.rem(gy + 7, 8)),
    )
    return x, y, z, core, at, beside


def share(block, produce, owner_ref, part, whole, from_core, sums, from_y, from_z, from_x, send, recv):
    x, y, z, core, at, _ = place()
    owner = owner_ref[block]
    owner_z = lax.div(owner, 8) * 2 + lax.div(lax.rem(owner, 8), 4)
    owner_x = lax.rem(owner, 4)
    y_at = lambda d: lax.rem(y + d, 4)
    z_at = lambda d: lax.rem(z + d, 8)
    to_core = at(0, 0, 0, 1)
    to_x = lambda d: at(d, 0, 0, 0)
    to_y = lambda d: at(0, d, 0, 0)
    to_z = lambda d: at(0, 0, d, 0)
    slot = [0]
    started = []

    def start(src, dst, device):
        number = slot[0]
        slot[0] += 1
        copy = pltpu.make_async_remote_copy(
            src_ref=src,
            dst_ref=dst,
            send_sem=send.at[block, number],
            recv_sem=recv.at[block, number],
            device_id=device,
            device_id_type=MESH,
        )
        copy.start()
        started.append(copy)
        return copy

    def arrive(copies):
        for copy in copies:
            copy.wait_recv()

    sent = []

    def pass_on(d, copy):
        copy.wait_recv()
        here = y_at(d)
        sums[here] = part[core, here] + from_core[here]
        if d > 0:
            sent.append(start(sums.at[here], from_y.at[d - 1], to_y(d)))

    before = None
    for d in (2, 1, 3, 0):
        produce(y_at(d))
        copy = start(part.at[1 - core, y_at(d)], from_core.at[y_at(d)], to_core)
        if before is not None:
            pass_on(*before)
        before = d, copy
    pass_on(*before)
    arrive(sent)
    sums[y] = sums[y] + from_y[0] + from_y[1] + from_y[2]

    far_first = (4, 3, 5, 2, 6, 1, 7)
    sent = [
        start(sums.at[y, pl.ds(z_at(d) * PIECE, PIECE)], from_z.at[z], to_z(d))
        for d in far_first
    ]
    mine = pl.ds(pl.multiple_of(z * PIECE, 8), PIECE)
    from_z[z] = sums[y, mine]
    arrive(sent)
    from_x[x] = from_z[owner_z]
    own = from_x.at[x]
    arrive([start(own, own, to_x(d)) for d in (2, 1, 3)])
    whole[core, y, mine] = from_x[owner_x]
    own = whole.at[core, y, mine]
    arrive([start(own, own, to_z(d)) for d in far_first])
    own = whole.at[core, y]
    sent = [start(own, own, to_y(d)) for d in (2, 1, 3)]
    flying = [start(own, own, to_core)]
    for d, copy in zip((2, 1, 3), sent):
        copy.wait_recv()
        came = whole.at[core, y_at(4 - d)]
        flying.append(start(came, came, to_core))
    arrive(flying)
    for copy in started:
        copy.wait_send()


N_COPIES = 4 + 3 + 7 + 3 + 7 + 3 + 4


def assimilate(
    block,
    owner_ref,
    error_ref,
    state,
    whole,
    observed_ref,
    column_x_ref,
    column_y_ref,
    peak_ref,
    spread,
    scaled,
    innovation,
    pert,
    solved_t,
    taper_y,
    taper_vx,
    system,
    weight,
    then,
):
    owner = owner_ref[block]
    one = slice(block, block + 1)
    inverses = [1.0 / jnp.full((1, 128), error_ref[channel], F32) for channel in range(NCH)]
    for channel in range(NCH):
        inverse = inverses[channel]
        for tile in range(4):
            half, quarter = tile // 2, tile % 2
            evolved = whole[half, channel, quarter * M : quarter * M + M, :]
            mean = jnp.sum(evolved, axis=0, keepdims=True) * (1.0 / M)
            lanes = slice(channel * NB + tile * 128, channel * NB + tile * 128 + 128)
            part = evolved - mean
            spread[:, lanes] = part
            pert[:, lanes] = part.astype(BF16)
            scaled[:M, lanes] = part * inverse
            away = observed_ref[block, channel : channel + 1, tile * 128 : tile * 128 + 128] - mean
            innovation[:, lanes] = away
            scaled[M:, lanes] = jnp.broadcast_to(away * inverse, (8, 128))
    cross = lax.dot_general(
        scaled[...], spread[...], (((1,), (1,)), ((), ())), precision=HIGHEST,
        preferred_element_type=F32,
    )
    lane = lax.broadcasted_iota(jnp.int32, (M + 8, 128), 1)
    row = lax.broadcasted_iota(jnp.int32, (M + 8, 128), 0)
    cross = jnp.concatenate([cross, jnp.zeros((M + 8, 128 - M), F32)], axis=1)
    system[...] = cross + jnp.where((lane == row) & (row < M), float(M - 1), 0.0)

    peak = peak_ref[one, :].astype(F32)
    at_x = lax.div(owner, 8) * CX + column_x_ref[one, :]
    at_y = lax.rem(owner, 8) * CY + column_y_ref[one, :]
    grid_y = lax.axis_index("gy") * CY + lax.broadcasted_iota(jnp.int32, (CY, NB), 0)
    gap = jnp.abs(grid_y - at_y)
    gap = jnp.minimum(gap, 8 * CY - gap).astype(F32)
    taper_y[...] = jnp.exp(-jnp.square(gap / HLOC_Y))
    index = lax.broadcasted_iota(jnp.int32, (ROWS, NB), 0)
    grid_x = lax.axis_index("gx") * CX + lax.rem(index, CX)
    gap = jnp.abs(grid_x - at_x)
    gap = jnp.minimum(gap, 4 * CX - gap).astype(F32)
    level = (lax.axis_index("lev") * LEV + lax.div(index, CX)).astype(F32)
    taper_vx[...] = (
        jnp.exp(-jnp.square((level - peak) / VLOC)) * jnp.exp(-jnp.square(gap / HLOC_X))
    ) * (1.0 / (M - 1))

    def sweep(pivot):
        matrix = system[...]
        pivot_row = system[pl.ds(pivot, 1), :]
        index = jnp.full((M + 8, 128), pivot, jnp.int32)
        column = jnp.take_along_axis(matrix, index, axis=1)
        corner = jnp.take_along_axis(jnp.broadcast_to(pivot_row, (8, 128)), index[:8], axis=1)[:1]
        at_row, at_lane = row == pivot, lane == pivot
        times = jnp.where(at_lane[:1], -1.0, pivot_row) * (1.0 / corner)
        column = jnp.where(at_row, -1.0, column)
        system[...] = jnp.where(at_row | at_lane, 0.0, matrix) - column * times

    @pl.loop(0, ROWS // GROUP)
    def _(group):
        for turn in range(STEPS):
            sweep(group * STEPS + turn)
        anomalies = []
        besides = []
        for at in range(GROUP):
            member = state[group * GROUP + at]
            anomaly = member - jnp.sum(member, axis=0, keepdims=True) * (1.0 / M)
            anomalies.append(anomaly.T.astype(BF16))
            besides.append(taper_vx[pl.ds(group * GROUP + at, 1), :])
        anomaly = jnp.concatenate(anomalies, axis=0)
        for chunk in range(NB // HALF):
            near = slice(chunk * HALF, chunk * HALF + HALF)
            taper = jnp.concatenate([taper_y[:, near] * b[:, near] for b in besides], axis=0)
            for channel in range(NCH):
                lanes = slice(channel * NB + chunk * HALF, channel * NB + chunk * HALF + HALF)
                covariance = jnp.dot(anomaly, pert[:, lanes], preferred_element_type=F32)
                rows = pl.ds(group * (GROUP * CY), GROUP * CY)
                weight[rows, lanes] = (taper * covariance).astype(BF16)

    swept = system[...]
    gain = (swept[M : M + 1] - 0.5 * (M - 1) * swept[:M])[:, :M]
    for channel in range(NCH):
        lanes = slice(channel * NB, channel * NB + NB)
        change = jnp.dot(gain, spread[:, lanes], precision=HIGHEST, preferred_element_type=F32)
        solved = inverses[channel][:, :1] * (innovation[:, lanes] - change)
        solved_t[lanes, :] = solved.T.astype(BF16)

    def finish(group):
        update = jnp.dot(
            weight[pl.ds(group * (LAST * CY), LAST * CY), :],
            solved_t[...],
            preferred_element_type=F32,
        )
        for at in range(LAST):
            here = group * LAST + at
            state[here] = state[here] + update[at * CY : at * CY + CY].T

    if then is None:
        pl.loop(0, ROWS // LAST)(finish)
    else:
        for group in range(ROWS // LAST):
            finish(group)
            then(group)


def transport(speed_x_ref, speed_y_ref, state, out_ref, middle, face, got, edge, came, send, recv):
    targets = place()[-1]
    lane = lax.broadcasted_iota(jnp.int32, (M, CY), 1)
    copies = {}

    def start(key, src, dst, target):
        number = len(copies)
        copies[key] = pltpu.make_async_remote_copy(
            src_ref=src,
            dst_ref=dst,
            send_sem=send.at[number],
            recv_sem=recv.at[number],
            device_id=target,
            device_id_type=MESH,
        )
        copies[key].start()

    def send_faces(turn, group):
        source = middle if turn else state
        for level in range(group * SOME, group * SOME + SOME):
            face[turn, 0, level] = source[level * CX + CX - 1].astype(BF16)
            face[turn, 1, level] = source[level * CX].astype(BF16)
        some = pl.ds(group * SOME, SOME)
        for n in range(2):
            start(
                ("x", turn, group, n), face.at[turn, n, some], got.at[turn, n, some], targets[n]
            )

    def send_edges(turn):
        source = middle if turn else state

        def pack(level, carry):
            last, first = carry
            for x in range(CX):
                tile = source[level * CX + x]
                here = lane == level * CX + x
                last = jnp.where(here, tile[:, CY - 1 :], last)
                first = jnp.where(here, tile[:, :1], first)
            return last, first

        nothing = jnp.zeros((M, CY), F32)
        edge[turn, 0], edge[turn, 1] = lax.fori_loop(0, LEV, pack, (nothing, nothing))
        for n in range(2):
            start(("y", turn, n), edge.at[turn, n], came.at[turn, n], targets[2 + n])

    def advance(turn, level):
        source = middle if turn else state
        shift = lax.rem(CY - level * CX, CY)
        souths = pltpu.roll(came[turn, 0], shift, 1)
        norths = pltpu.roll(came[turn, 1], shift, 1)
        for x in range(CX):
            at = level * CX + x
            centre = source[at]
            west = source[at - 1] if x > 0 else got[turn, 0, level].astype(F32)
            east = source[at + 1] if x < CX - 1 else got[turn, 1, level].astype(F32)
            south = jnp.where(lane == 0, souths[:, x : x + 1], pltpu.roll(centre, 1, 1))
            north = jnp.where(lane == CY - 1, norths[:, x : x + 1], pltpu.roll(centre, CY - 1, 1))
            u = speed_x_ref[pl.ds(at, 1), :]
            v = speed_y_ref[pl.ds(at, 1), :]
            value = (
                centre * (1.0 - 4.0 * KAPPA - jnp.abs(u) - jnp.abs(v))
                + west * (jnp.maximum(u, 0.0) + KAPPA)
                + east * (KAPPA - jnp.minimum(u, 0.0))
                + south * (jnp.maximum(v, 0.0) + KAPPA)
                + north * (KAPPA - jnp.minimum(v, 0.0))
            )
            if turn == 0:
                middle[at] = value
            else:
                out_ref[pl.ds(at, M, stride=ROWS), :] = value

    def rest():
        for turn in range(2):
            send_edges(turn)
            for n in range(2):
                copies["y", turn, n].wait_recv()
            for group in range(LEV // SOME):
                for n in range(2):
                    copies["x", turn, group, n].wait_recv()
                pl.loop(group * SOME, group * SOME + SOME)(lambda level: advance(turn, level))
                if turn == 0:
                    send_faces(1, group)
        for copy in copies.values():
            copy.wait_send()

    return send_faces, rest


def filter_kernel(
    scale_ref,
    weight_ref,
    error_ref,
    owner_ref,
    ensemble_ref,
    observed_ref,
    column_x_ref,
    column_y_ref,
    peak_ref,
    speed_x_ref,
    speed_y_ref,
    out_ref,
    state,
    gathered,
    part,
    whole_0,
    whole_1,
    from_core_0,
    from_core_1,
    sums,
    from_y_0,
    from_y_1,
    from_z_0,
    from_z_1,
    from_x_0,
    from_x_1,
    spread,
    scaled,
    innovation,
    pert,
    solved_t,
    taper_y,
    taper_vx,
    system,
    weight,
    middle,
    face,
    got,
    edge,
    came,
    send,
    recv,
    face_send,
    face_recv,
):
    at, beside = place()[-2:]
    peers = [at(0, 0, 0, 1)] + [at(0, d, 0, 0) for d in range(1, 4)]
    peers += [at(0, 0, d, 0) for d in range(1, 8)] + [at(d, 0, 0, 0) for d in range(1, 4)]
    peers += beside
    barrier = pltpu.get_barrier_semaphore()
    for peer in peers:
        pl.semaphore_signal(barrier, inc=1, device_id=peer, device_id_type=MESH)

    for row in range(ROWS):
        state[row] = ensemble_ref[pl.ds(row, M, stride=ROWS), :]
    send_faces, rest = transport(
        speed_x_ref, speed_y_ref, state, out_ref, middle, face, got, edge, came, face_send,
        face_recv,
    )
    for block in range(NBLK):
        produce = radiances(
            block, scale_ref, weight_ref, state, column_x_ref, column_y_ref, peak_ref, part,
            gathered,
        )
        if block == 0:
            pl.semaphore_wait(barrier, len(peers))
        whole = (whole_0, whole_1)[block]
        from_core = (from_core_0, from_core_1)[block]
        from_y = (from_y_0, from_y_1)[block]
        from_z = (from_z_0, from_z_1)[block]
        from_x = (from_x_0, from_x_1)[block]
        share(
            block, produce, owner_ref, part, whole, from_core, sums, from_y, from_z, from_x, send,
            recv,
        )
        then = None if block < NBLK - 1 else lambda group: send_faces(0, group)
        assimilate(
            block, owner_ref, error_ref, state, whole, observed_ref, column_x_ref, column_y_ref,
            peak_ref, spread, scaled, innovation, pert, solved_t, taper_y, taper_vx, system, weight,
            then,
        )
    rest()


SMEM_SPEC = pl.BlockSpec(memory_space=pltpu.SMEM)
VMEM_SPEC = pl.BlockSpec(memory_space=pltpu.VMEM)


def shards(
    ensemble,
    level_scale,
    channel_weights,
    error_var,
    observed,
    column_x,
    column_y,
    peak_level,
    owner_map,
    courant_x,
    courant_y,
):
    result = pl.pallas_call(
        filter_kernel,
        out_shape=jax.ShapeDtypeStruct((M * ROWS, CY), F32),
        in_specs=[SMEM_SPEC] * 4 + [VMEM_SPEC] * 7,
        out_specs=VMEM_SPEC,
        scratch_shapes=[
            pltpu.VMEM((ROWS, M, CY), F32),
            pltpu.VMEM((LEV, M, NB), F32),
            pltpu.VMEM((2, NCH, 2 * M, 128), F32),
            *[pltpu.VMEM((2, NCH, 2 * M, 128), F32)] * NBLK,
            *[pltpu.VMEM((4, 2 * M, 128), F32)] * NBLK,
            pltpu.VMEM((4, 2 * M, 128), F32),
            *[pltpu.VMEM((3, 2 * M, 128), F32)] * NBLK,
            *[pltpu.VMEM((8, PIECE, 128), F32)] * NBLK,
            *[pltpu.VMEM((4, PIECE, 128), F32)] * NBLK,
            pltpu.VMEM((M, NCH * NB), F32),
            pltpu.VMEM((M + 8, NCH * NB), F32),
            pltpu.VMEM((1, NCH * NB), F32),
            pltpu.VMEM((M, NCH * NB), BF16),
            pltpu.VMEM((NCH * NB, M), BF16),
            pltpu.VMEM((CY, NB), F32),
            pltpu.VMEM((ROWS, NB), F32),
            pltpu.VMEM((M + 8, 128), F32),
            pltpu.VMEM((ROWS * CY, NCH * NB), BF16),
            pltpu.VMEM((ROWS, M, CY), F32),
            pltpu.VMEM((2, 2, LEV, M, CY), BF16),
            pltpu.VMEM((2, 2, LEV, M, CY), BF16),
            pltpu.VMEM((2, 2, M, CY), F32),
            pltpu.VMEM((2, 2, M, CY), F32),
            pltpu.SemaphoreType.DMA((NBLK, N_COPIES)),
            pltpu.SemaphoreType.DMA((NBLK, N_COPIES)),
            pltpu.SemaphoreType.DMA((N_FACES,)),
            pltpu.SemaphoreType.DMA((N_FACES,)),
        ],
        compiler_params=pltpu.CompilerParams(
            vmem_limit_bytes=VMEM_LIMIT, collective_id=0, has_side_effects=True
        ),
        name="filter",
    )(
        level_scale,
        channel_weights,
        error_var,
        owner_map,
        ensemble.reshape(M * ROWS, CY),
        observed,
        column_x,
        column_y,
        peak_level,
        courant_x.reshape(ROWS, CY),
        courant_y.reshape(ROWS, CY),
    )
    return result.reshape(ensemble.shape)


def solution(mesh):
    in_specs = (
        P(None, "lev", "gx", "gy"),
        P("lev"),
        P(None, "lev"),
        P(),
        P(),
        P(),
        P(),
        P(),
        P(),
        P("lev", "gx", "gy"),
        P("lev", "gx", "gy"),
    )
    out_specs = P(None, "lev", "gx", "gy")
    return jax.shard_map(shards, mesh=mesh, in_specs=in_specs, out_specs=out_specs, check_vma=False)
```

time: 968 us -> 137 us (0.14)
  waiting for transfers between devices: 459 us -> 0 us
  local copies, waits for them, and re-layouts: 164 us -> 2.67 us
  other arithmetic: 155 us -> 0 us
  Pallas kernels: 0 us -> 132 us
  matrix products: 125 us -> 0 us
  loops' own time: 23.2 us -> 0 us
  between operations: 20.5 us -> 0.01 us
  starting transfers between devices: 13.9 us -> 0 us
    psum x4 -> x0, waiting for transfers between devices: 422 us -> none  [the longest x2 290 us: from_root(): return lax.psum(jnp.where(mine, shard, jnp.zeros_like(shard)), axis)]
    pallas_call x0 -> x1, Pallas kernels: none -> 132 us  [shards(): pl.pallas_call(filter_kernel, out_shape=jax.ShapeDtypeStruct((M * ROWS, C...]
    dot_general x40 -> x0, matrix products: 124 us -> none  [the longest x32 103 us: one_sub(): lax.dot_general(solved_sub, weight, (((1,), (1,)), ((), ())), preferred_e...]
    mul x64 -> x0, other arithmetic: 77.6 us -> none  [one_sub(): taper_v[:, None, None, :] * taper_x[None, :, None, :]]
    mul x32 -> x0, local copies, waits for them, and re-layouts: 67.3 us -> none  [one_sub(): taper_v[:, None, None, :] * taper_x[None, :, None, :]]
    ppermute x8 -> x0, waiting for transfers between devices: 36.9 us -> none  [the longest x4 25 us: padded_2(): lax.ppermute(head, axis, [((i + 1) % count, i) for i in range(count)])]
    another operation x10 -> x0, other arithmetic: 34.9 us -> none  [the longest x6 18.9 us: solve_spd(): factor = jnp.linalg.cholesky(matrix)]
    dynamic_slice x128 -> x0, local copies, waits for them, and re-layouts: 28.2 us -> none  [the longest x32 20.9 us: shards(): lax.scan(one_sub, start_sum, jnp.arange(piece_width // sub_width, dtype=j...]
  transfers between devices with their start and end apart: 12 -> 0, of which waited for: 9 -> 0; matrix products, arithmetic and copies ran while one was open for 2% -> 0% of each run, Pallas kernels for 0% -> 0%
where the time goes in v2:
time: 137 us; the launch traced here: 135 us
  Pallas kernels  132 us (96%)
  local copies, waits for them, and re-layouts  2.67 us (2%)
    pallas_call x1, Pallas kernels, shards(): pl.pallas_call(filter_kernel, out_shape=jax.ShapeDtypeStruct((M * ROWS, C...  132 us

profile of v2, /device:TPU:32, one launch (start us, length us, event | category | flops | bytes accessed | tf_op | source)
XLA Modules:
  0.0 135.1 jit_solution(12572686742297482847)
XLA Ops:
  0.0 132.4 %filter.1 = f32[3072,128]{1,0:T(8,128)} custom-call(f32[8]{0:T(128)} %scale_ref.1, f32[4,8]{1,0:T(4,128)} %weight_ref.1, f32[4]{0:T(128)} %error_ref.1, s32[2]{0:T(128)} %owner_ref.1, f32[3072,128]{1,0:T(8,128)} %bitcast.5, f32[2,4,512]{2,1,0:T(4,128)} %observed_ref.1, s32[2,512]{1,0:T(2,128)} %column_x_ref.1, s32[2,512]{1,0:T(2,128)} %column_y_ref.1, ...), custom_call_target="tpu_custom_call" | custom-call | tf_op jit(solution)/shard_map/filter/pallas_call | solution.py:493
  132.4 2.7 %copy.13 = f32[96,8,4,128]{3,2,1,0:T(4,128)} copy(f32[96,8,4,128]{3,2,1,0:T(4,128)} %bitcast.4) | data formatting | bytes 3145728

commit v3 on v2

--- a/solution.py
+++ b/solution.py
@@ -23,10 +23,10 @@
 HALF = 256
 GROUP = 4
 LAST = 8
-STEPS = M // ROWS * GROUP
+STEPS = M // ROWS * GROUP // 2
 PIECE = 24
-SOME = LAST // CX
-N_FACES = 2 * (2 * (LEV // SOME) + 2)
+SOME = LEV // 2
+N_FACES = 2 * (2 * 2 + 2 * 2)
 
 F32 = jnp.float32
 BF16 = jnp.bfloat16
@@ -72,6 +72,10 @@
             part[half, channel, quarter * M : quarter * M + M, :] = total
 
     return produce
+
+
+def row_of(kind, level, which):
+    return level * CX + which * (3 - 2 * kind) + kind
 
 
 def place():
@@ -242,16 +246,30 @@
         jnp.exp(-jnp.square((level - peak) / VLOC)) * jnp.exp(-jnp.square(gap / HLOC_X))
     ) * (1.0 / (M - 1))
 
-    def sweep(pivot):
+    def sweep(pair):
+        p, q = pair * 2, pair * 2 + 1
         matrix = system[...]
-        pivot_row = system[pl.ds(pivot, 1), :]
-        index = jnp.full((M + 8, 128), pivot, jnp.int32)
-        column = jnp.take_along_axis(matrix, index, axis=1)
-        corner = jnp.take_along_axis(jnp.broadcast_to(pivot_row, (8, 128)), index[:8], axis=1)[:1]
-        at_row, at_lane = row == pivot, lane == pivot
-        times = jnp.where(at_lane[:1], -1.0, pivot_row) * (1.0 / corner)
-        column = jnp.where(at_row, -1.0, column)
-        system[...] = jnp.where(at_row | at_lane, 0.0, matrix) - column * times
+        row_p, row_q = system[pl.ds(p, 1), :], system[pl.ds(q, 1), :]
+        at_p, at_q = jnp.full((M + 8, 128), p, jnp.int32), jnp.full((M + 8, 128), q, jnp.int32)
+        column_p = jnp.take_along_axis(matrix, at_p, axis=1)
+        column_q = jnp.take_along_axis(matrix, at_q, axis=1)
+        rows_p, rows_q = jnp.broadcast_to(row_p, (8, 128)), jnp.broadcast_to(row_q, (8, 128))
+        pp = jnp.take_along_axis(rows_p, at_p[:8], axis=1)[:1]
+        pq = jnp.take_along_axis(rows_p, at_q[:8], axis=1)[:1]
+        qq = jnp.take_along_axis(rows_q, at_q[:8], axis=1)[:1]
+        inverse = 1.0 / (pp * qq - pq * pq)
+        lane_p, lane_q = lane == p, lane == q
+        away = lane_p[:1] | lane_q[:1]
+        row_p = jnp.where(away, jnp.where(lane_p[:1], -1.0, 0.0), row_p)
+        row_q = jnp.where(away, jnp.where(lane_q[:1], -1.0, 0.0), row_q)
+        times_p = (qq * inverse) * row_p - (pq * inverse) * row_q
+        times_q = (pp * inverse) * row_q - (pq * inverse) * row_p
+        is_p, is_q = row == p, row == q
+        swept = is_p | is_q
+        column_p = jnp.where(swept, jnp.where(is_p, -1.0, 0.0), column_p)
+        column_q = jnp.where(swept, jnp.where(is_q, -1.0, 0.0), column_q)
+        matrix = jnp.where(swept | lane_p | lane_q, 0.0, matrix)
+        system[...] = matrix - column_p * times_p - column_q * times_q
 
     @pl.loop(0, ROWS // GROUP)
     def _(group):
@@ -260,10 +278,11 @@
         anomalies = []
         besides = []
         for at in range(GROUP):
-            member = state[group * GROUP + at]
+            here = row_of(lax.div(group, 4), lax.rem(group, 4) * (GROUP // 2) + at // 2, at % 2)
+            member = state[here]
             anomaly = member - jnp.sum(member, axis=0, keepdims=True) * (1.0 / M)
             anomalies.append(anomaly.T.astype(BF16))
-            besides.append(taper_vx[pl.ds(group * GROUP + at, 1), :])
+            besides.append(taper_vx[pl.ds(here, 1), :])
         anomaly = jnp.concatenate(anomalies, axis=0)
         for chunk in range(NB // HALF):
             near = slice(chunk * HALF, chunk * HALF + HALF)
@@ -289,14 +308,12 @@
             preferred_element_type=F32,
         )
         for at in range(LAST):
-            here = group * LAST + at
+            here = row_of(group // 2, group % 2 * (LAST // 2) + at // 2, at % 2)
             state[here] = state[here] + update[at * CY : at * CY + CY].T
 
-    if then is None:
-        pl.loop(0, ROWS // LAST)(finish)
-    else:
-        for group in range(ROWS // LAST):
-            finish(group)
+    for group in range(ROWS // LAST):
+        finish(group)
+        if then is not None:
             then(group)
 
 
@@ -317,46 +334,57 @@
         )
         copies[key].start()
 
-    def send_faces(turn, group):
+    def send_faces(turn, half):
         source = middle if turn else state
-        for level in range(group * SOME, group * SOME + SOME):
+        for level in range(half * SOME, half * SOME + SOME):
             face[turn, 0, level] = source[level * CX + CX - 1].astype(BF16)
             face[turn, 1, level] = source[level * CX].astype(BF16)
-        some = pl.ds(group * SOME, SOME)
+        some = pl.ds(half * SOME, SOME)
+        for n in range(2):
+            start(("x", turn, half, n), face.at[turn, n, some], got.at[turn, n, some], targets[n])
+
+    def send_edges(turn, kind):
+        source = middle if turn else state
+
+        def pack(level, packed):
+            for which in range(2):
+                slot = level * 2 + which
+                turned = pltpu.roll(source[row_of(kind, level, which)], slot * 2 + 2, 1)
+                here = (lane == slot * 2 + 1) | (lane == slot * 2 + 2)
+                packed = jnp.where(here, turned, packed)
+            return packed
+
+        edge[turn, kind] = lax.fori_loop(0, LEV, pack, jnp.zeros((M, CY), F32))
         for n in range(2):
             start(
-                ("x", turn, group, n), face.at[turn, n, some], got.at[turn, n, some], targets[n]
+                ("y", turn, kind, n), edge.at[turn, kind], came.at[turn, kind, n], targets[2 + n]
             )
 
-    def send_edges(turn):
+    def take_edges(turn, kind):
+        for n in range(2):
+            copies["y", turn, kind, n].wait_recv()
+        return jnp.where(
+            lax.rem(lane, 2) == 1,
+            came[turn, kind, 0],
+            pltpu.roll(came[turn, kind, 1], CY - 2, 1),
+        )
+
+    def advance(turn, kind, edges, level):
         source = middle if turn else state
-
-        def pack(level, carry):
-            last, first = carry
-            for x in range(CX):
-                tile = source[level * CX + x]
-                here = lane == level * CX + x
-                last = jnp.where(here, tile[:, CY - 1 :], last)
-                first = jnp.where(here, tile[:, :1], first)
-            return last, first
-
-        nothing = jnp.zeros((M, CY), F32)
-        edge[turn, 0], edge[turn, 1] = lax.fori_loop(0, LEV, pack, (nothing, nothing))
-        for n in range(2):
-            start(("y", turn, n), edge.at[turn, n], came.at[turn, n], targets[2 + n])
-
-    def advance(turn, level):
-        source = middle if turn else state
-        shift = lax.rem(CY - level * CX, CY)
-        souths = pltpu.roll(came[turn, 0], shift, 1)
-        norths = pltpu.roll(came[turn, 1], shift, 1)
-        for x in range(CX):
-            at = level * CX + x
+        for which in range(2):
+            at = row_of(kind, level, which)
             centre = source[at]
-            west = source[at - 1] if x > 0 else got[turn, 0, level].astype(F32)
-            east = source[at + 1] if x < CX - 1 else got[turn, 1, level].astype(F32)
-            south = jnp.where(lane == 0, souths[:, x : x + 1], pltpu.roll(centre, 1, 1))
-            north = jnp.where(lane == CY - 1, norths[:, x : x + 1], pltpu.roll(centre, CY - 1, 1))
+            if kind == 0 and which == 0:
+                west = got[turn, 0, level].astype(F32)
+            else:
+                west = source[at - 1]
+            if kind == 0 and which == 1:
+                east = got[turn, 1, level].astype(F32)
+            else:
+                east = source[at + 1]
+            beyond = pltpu.roll(edges, CY - 1 - 2 * (level * 2 + which), 1)
+            south = jnp.where(lane == 0, beyond, pltpu.roll(centre, 1, 1))
+            north = jnp.where(lane == CY - 1, beyond, pltpu.roll(centre, CY - 1, 1))
             u = speed_x_ref[pl.ds(at, 1), :]
             v = speed_y_ref[pl.ds(at, 1), :]
             value = (
@@ -371,21 +399,40 @@
             else:
                 out_ref[pl.ds(at, M, stride=ROWS), :] = value
 
+    def levels(turn, kind, edges, first, last):
+        pl.loop(first, last)(lambda level: advance(turn, kind, edges, level))
+
+    def outer(turn):
+        edges = take_edges(turn, 0)
+        for half in range(LEV // SOME):
+            for n in range(2):
+                copies["x", turn, half, n].wait_recv()
+            levels(turn, 0, edges, half * SOME, half * SOME + SOME)
+            if turn == 0:
+                send_faces(1, half)
+
+    def inner(turn):
+        levels(turn, 1, take_edges(turn, 1), 0, LEV)
+
+    def early(group):
+        if group < 2:
+            send_faces(0, group)
+        if group == 1:
+            send_edges(0, 0)
+        if group == 3:
+            send_edges(0, 1)
+
     def rest():
-        for turn in range(2):
-            send_edges(turn)
-            for n in range(2):
-                copies["y", turn, n].wait_recv()
-            for group in range(LEV // SOME):
-                for n in range(2):
-                    copies["x", turn, group, n].wait_recv()
-                pl.loop(group * SOME, group * SOME + SOME)(lambda level: advance(turn, level))
-                if turn == 0:
-                    send_faces(1, group)
+        outer(0)
+        send_edges(1, 0)
+        inner(0)
+        send_edges(1, 1)
+        inner(1)
+        outer(1)
         for copy in copies.values():
             copy.wait_send()
 
-    return send_faces, rest
+    return early, rest
 
 
 def filter_kernel(
@@ -444,7 +491,7 @@
 
     for row in range(ROWS):
         state[row] = ensemble_ref[pl.ds(row, M, stride=ROWS), :]
-    send_faces, rest = transport(
+    early, rest = transport(
         speed_x_ref, speed_y_ref, state, out_ref, middle, face, got, edge, came, face_send,
         face_recv,
     )
@@ -464,7 +511,7 @@
             block, produce, owner_ref, part, whole, from_core, sums, from_y, from_z, from_x, send,
             recv,
         )
-        then = None if block < NBLK - 1 else lambda group: send_faces(0, group)
+        then = None if block < NBLK - 1 else early
         assimilate(
             block, owner_ref, error_ref, state, whole, observed_ref, column_x_ref, column_y_ref,
             peak_ref, spread, scaled, innovation, pert, solved_t, taper_y, taper_vx, system, weight,
@@ -518,7 +565,7 @@
             pltpu.VMEM((2, 2, LEV, M, CY), BF16),
             pltpu.VMEM((2, 2, LEV, M, CY), BF16),
             pltpu.VMEM((2, 2, M, CY), F32),
-            pltpu.VMEM((2, 2, M, CY), F32),
+            pltpu.VMEM((2, 2, 2, M, CY), F32),
             pltpu.SemaphoreType.DMA((NBLK, N_COPIES)),
             pltpu.SemaphoreType.DMA((NBLK, N_COPIES)),
             pltpu.SemaphoreType.DMA((N_FACES,)),

time: 137 us -> 130 us (0.949)
  Pallas kernels: 132 us -> 126 us
    pallas_call x1, Pallas kernels: 132 us -> 126 us  [shards(): pl.pallas_call(filter_kernel, out_shape=jax.ShapeDtypeStruct((M * ROWS, C...]
where the time goes in v3:
time: 130 us; the launch traced here: 129 us
  Pallas kernels  126 us (97%)
  local copies, waits for them, and re-layouts  2.67 us (2%)
    pallas_call x1, Pallas kernels, shards(): pl.pallas_call(filter_kernel, out_shape=jax.ShapeDtypeStruct((M * ROWS, C...  126 us
    unnamed x1, local copies, waits for them, and re-layouts  2.67 us

profile of v3, /device:TPU:32, one launch (start us, length us, event | category | flops | bytes accessed | tf_op | source)
XLA Modules:
  0.0 128.6 jit_solution(16066765278654108164)
XLA Ops:
  0.0 125.9 %filter.1 = f32[3072,128]{1,0:T(8,128)} custom-call(f32[8]{0:T(128)} %scale_ref.1, f32[4,8]{1,0:T(4,128)} %weight_ref.1, f32[4]{0:T(128)} %error_ref.1, s32[2]{0:T(128)} %owner_ref.1, f32[3072,128]{1,0:T(8,128)} %bitcast.5, f32[2,4,512]{2,1,0:T(4,128)} %observed_ref.1, s32[2,512]{1,0:T(2,128)} %column_x_ref.1, s32[2,512]{1,0:T(2,128)} %column_y_ref.1, ...), custom_call_target="tpu_custom_call" | custom-call | tf_op jit(solution)/shard_map/filter/pallas_call | solution.py:540
  125.9 2.7 %copy.13 = f32[96,8,4,128]{3,2,1,0:T(4,128)} copy(f32[96,8,4,128]{3,2,1,0:T(4,128)} %bitcast.4) | data formatting | bytes 3145728

commit v4 on v3

--- a/solution.py
+++ b/solution.py
@@ -101,7 +101,7 @@
     return x, y, z, core, at, beside
 
 
-def share(block, produce, owner_ref, part, whole, from_core, sums, from_y, from_z, from_x, send, recv):
+def share(block, enter, produce, meanwhile, digest, owner_ref, part, whole, from_core, sums, from_y, from_z, from_x, send, recv):
     x, y, z, core, at, _ = place()
     owner = owner_ref[block]
     owner_z = lax.div(owner, 8) * 2 + lax.div(lax.rem(owner, 8), 4)
@@ -144,8 +144,15 @@
             sent.append(start(sums.at[here], from_y.at[d - 1], to_y(d)))
 
     before = None
-    for d in (2, 1, 3, 0):
-        produce(y_at(d))
+    order = (2, 1, 3, 0)
+    if enter is not None:
+        for d in order:
+            produce(y_at(d))
+        meanwhile()
+        enter()
+    for d in order:
+        if enter is None:
+            produce(y_at(d))
         copy = start(part.at[1 - core, y_at(d)], from_core.at[y_at(d)], to_core)
         if before is not None:
             pass_on(*before)
@@ -161,6 +168,8 @@
     ]
     mine = pl.ds(pl.multiple_of(z * PIECE, 8), PIECE)
     from_z[z] = sums[y, mine]
+    if enter is None:
+        meanwhile()
     arrive(sent)
     from_x[x] = from_z[owner_z]
     own = from_x.at[x]
@@ -169,15 +178,18 @@
     own = whole.at[core, y, mine]
     arrive([start(own, own, to_z(d)) for d in far_first])
     own = whole.at[core, y]
-    sent = [start(own, own, to_y(d)) for d in (2, 1, 3)]
-    flying = [start(own, own, to_core)]
-    for d, copy in zip((2, 1, 3), sent):
-        copy.wait_recv()
+    sent = {d: start(own, own, to_y(d)) for d in (2, 1, 3)}
+    before = start(own, own, to_core), y
+    for d in (1, 3, 2):
+        sent[d].wait_recv()
         came = whole.at[core, y_at(4 - d)]
-        flying.append(start(came, came, to_core))
-    arrive(flying)
-    for copy in started:
-        copy.wait_send()
+        after = start(came, came, to_core), y_at(4 - d)
+        before[0].wait_recv()
+        digest(before[1])
+        before = after
+    before[0].wait_recv()
+    digest(before[1])
+    return started
 
 
 N_COPIES = 4 + 3 + 7 + 3 + 7 + 3 + 4
@@ -202,49 +214,62 @@
     taper_vx,
     system,
     weight,
+    share_now,
     then,
 ):
     owner = owner_ref[block]
     one = slice(block, block + 1)
-    inverses = [1.0 / jnp.full((1, 128), error_ref[channel], F32) for channel in range(NCH)]
-    for channel in range(NCH):
-        inverse = inverses[channel]
+    cross = []
+
+    def inverse_of(channel):
+        return 1.0 / jnp.full((1, 128), error_ref[channel], F32)
+
+    def digest(channel):
+        inverse = inverse_of(channel)
+        this = lax.broadcasted_iota(jnp.int32, (NCH, 128), 0) == channel
         for tile in range(4):
             half, quarter = tile // 2, tile % 2
             evolved = whole[half, channel, quarter * M : quarter * M + M, :]
             mean = jnp.sum(evolved, axis=0, keepdims=True) * (1.0 / M)
-            lanes = slice(channel * NB + tile * 128, channel * NB + tile * 128 + 128)
+            lanes = slice(tile * 128, tile * 128 + 128)
             part = evolved - mean
-            spread[:, lanes] = part
-            pert[:, lanes] = part.astype(BF16)
+            spread[channel, :, lanes] = part
+            pert[channel, :, lanes] = part.astype(BF16)
             scaled[:M, lanes] = part * inverse
-            away = observed_ref[block, channel : channel + 1, tile * 128 : tile * 128 + 128] - mean
-            innovation[:, lanes] = away
+            wanted = jnp.where(this, observed_ref[block, :, lanes], 0.0)
+            away = jnp.sum(wanted, axis=0, keepdims=True) - mean
+            innovation[channel, :, lanes] = away
             scaled[M:, lanes] = jnp.broadcast_to(away * inverse, (8, 128))
-    cross = lax.dot_general(
-        scaled[...], spread[...], (((1,), (1,)), ((), ())), precision=HIGHEST,
-        preferred_element_type=F32,
-    )
+        cross.append(
+            lax.dot_general(
+                scaled[...], spread[channel], (((1,), (1,)), ((), ())), precision=HIGHEST,
+                preferred_element_type=F32,
+            )
+        )
+
+    def tapers():
+        peak = peak_ref[one, :].astype(F32)
+        at_x = lax.div(owner, 8) * CX + column_x_ref[one, :]
+        at_y = lax.rem(owner, 8) * CY + column_y_ref[one, :]
+        grid_y = lax.axis_index("gy") * CY + lax.broadcasted_iota(jnp.int32, (CY, NB), 0)
+        gap = jnp.abs(grid_y - at_y)
+        gap = jnp.minimum(gap, 8 * CY - gap).astype(F32)
+        taper_y[...] = jnp.exp(-jnp.square(gap / HLOC_Y))
+        index = lax.broadcasted_iota(jnp.int32, (ROWS, NB), 0)
+        grid_x = lax.axis_index("gx") * CX + lax.rem(index, CX)
+        gap = jnp.abs(grid_x - at_x)
+        gap = jnp.minimum(gap, 4 * CX - gap).astype(F32)
+        level = (lax.axis_index("lev") * LEV + lax.div(index, CX)).astype(F32)
+        taper_vx[...] = (
+            jnp.exp(-jnp.square((level - peak) / VLOC)) * jnp.exp(-jnp.square(gap / HLOC_X))
+        ) * (1.0 / (M - 1))
+
+    started = share_now(tapers, digest)
+    cross = cross[0] + cross[1] + cross[2] + cross[3]
     lane = lax.broadcasted_iota(jnp.int32, (M + 8, 128), 1)
     row = lax.broadcasted_iota(jnp.int32, (M + 8, 128), 0)
     cross = jnp.concatenate([cross, jnp.zeros((M + 8, 128 - M), F32)], axis=1)
     system[...] = cross + jnp.where((lane == row) & (row < M), float(M - 1), 0.0)
-
-    peak = peak_ref[one, :].astype(F32)
-    at_x = lax.div(owner, 8) * CX + column_x_ref[one, :]
-    at_y = lax.rem(owner, 8) * CY + column_y_ref[one, :]
-    grid_y = lax.axis_index("gy") * CY + lax.broadcasted_iota(jnp.int32, (CY, NB), 0)
-    gap = jnp.abs(grid_y - at_y)
-    gap = jnp.minimum(gap, 8 * CY - gap).astype(F32)
-    taper_y[...] = jnp.exp(-jnp.square(gap / HLOC_Y))
-    index = lax.broadcasted_iota(jnp.int32, (ROWS, NB), 0)
-    grid_x = lax.axis_index("gx") * CX + lax.rem(index, CX)
-    gap = jnp.abs(grid_x - at_x)
-    gap = jnp.minimum(gap, 4 * CX - gap).astype(F32)
-    level = (lax.axis_index("lev") * LEV + lax.div(index, CX)).astype(F32)
-    taper_vx[...] = (
-        jnp.exp(-jnp.square((level - peak) / VLOC)) * jnp.exp(-jnp.square(gap / HLOC_X))
-    ) * (1.0 / (M - 1))
 
     def sweep(pair):
         p, q = pair * 2, pair * 2 + 1
@@ -289,7 +314,9 @@
             taper = jnp.concatenate([taper_y[:, near] * b[:, near] for b in besides], axis=0)
             for channel in range(NCH):
                 lanes = slice(channel * NB + chunk * HALF, channel * NB + chunk * HALF + HALF)
-                covariance = jnp.dot(anomaly, pert[:, lanes], preferred_element_type=F32)
+                covariance = jnp.dot(
+                    anomaly, pert[channel, :, near], preferred_element_type=F32
+                )
                 rows = pl.ds(group * (GROUP * CY), GROUP * CY)
                 weight[rows, lanes] = (taper * covariance).astype(BF16)
 
@@ -297,8 +324,8 @@
     gain = (swept[M : M + 1] - 0.5 * (M - 1) * swept[:M])[:, :M]
     for channel in range(NCH):
         lanes = slice(channel * NB, channel * NB + NB)
-        change = jnp.dot(gain, spread[:, lanes], precision=HIGHEST, preferred_element_type=F32)
-        solved = inverses[channel][:, :1] * (innovation[:, lanes] - change)
+        change = jnp.dot(gain, spread[channel], precision=HIGHEST, preferred_element_type=F32)
+        solved = inverse_of(channel)[:, :1] * (innovation[channel] - change)
         solved_t[lanes, :] = solved.T.astype(BF16)
 
     def finish(group):
@@ -315,6 +342,8 @@
         finish(group)
         if then is not None:
             then(group)
+    for copy in started:
+        copy.wait_send()
 
 
 def transport(speed_x_ref, speed_y_ref, state, out_ref, middle, face, got, edge, came, send, recv):
@@ -374,45 +403,46 @@
         for which in range(2):
             at = row_of(kind, level, which)
             centre = source[at]
-            if kind == 0 and which == 0:
-                west = got[turn, 0, level].astype(F32)
-            else:
-                west = source[at - 1]
-            if kind == 0 and which == 1:
-                east = got[turn, 1, level].astype(F32)
-            else:
-                east = source[at + 1]
+            u = speed_x_ref[pl.ds(at, 1), :]
+            v = speed_y_ref[pl.ds(at, 1), :]
+            value = centre * (1.0 - 4.0 * KAPPA - jnp.abs(u) - jnp.abs(v))
+            if kind == 1 or which == 1:
+                value += source[at - 1] * (jnp.maximum(u, 0.0) + KAPPA)
+            if kind == 1 or which == 0:
+                value += source[at + 1] * (KAPPA - jnp.minimum(u, 0.0))
             beyond = pltpu.roll(edges, CY - 1 - 2 * (level * 2 + which), 1)
             south = jnp.where(lane == 0, beyond, pltpu.roll(centre, 1, 1))
             north = jnp.where(lane == CY - 1, beyond, pltpu.roll(centre, CY - 1, 1))
-            u = speed_x_ref[pl.ds(at, 1), :]
-            v = speed_y_ref[pl.ds(at, 1), :]
-            value = (
-                centre * (1.0 - 4.0 * KAPPA - jnp.abs(u) - jnp.abs(v))
-                + west * (jnp.maximum(u, 0.0) + KAPPA)
-                + east * (KAPPA - jnp.minimum(u, 0.0))
-                + south * (jnp.maximum(v, 0.0) + KAPPA)
-                + north * (KAPPA - jnp.minimum(v, 0.0))
-            )
+            value += south * (jnp.maximum(v, 0.0) + KAPPA) + north * (KAPPA - jnp.minimum(v, 0.0))
             if turn == 0:
                 middle[at] = value
+            elif kind == 0:
+                state[at] = value
             else:
                 out_ref[pl.ds(at, M, stride=ROWS), :] = value
 
-    def levels(turn, kind, edges, first, last):
-        pl.loop(first, last)(lambda level: advance(turn, kind, edges, level))
+    def complete(turn, level):
+        for which in range(2):
+            at = row_of(0, level, which)
+            u = speed_x_ref[pl.ds(at, 1), :]
+            factor = KAPPA - jnp.minimum(u, 0.0) if which else jnp.maximum(u, 0.0) + KAPPA
+            term = got[turn, which, level].astype(F32) * factor
+            if turn == 0:
+                middle[at] = middle[at] + term
+            else:
+                out_ref[pl.ds(at, M, stride=ROWS), :] = state[at] + term
+
+    def alone(turn, kind):
+        edges = take_edges(turn, kind)
+        pl.loop(0, LEV)(lambda level: advance(turn, kind, edges, level))
 
     def outer(turn):
-        edges = take_edges(turn, 0)
         for half in range(LEV // SOME):
             for n in range(2):
                 copies["x", turn, half, n].wait_recv()
-            levels(turn, 0, edges, half * SOME, half * SOME + SOME)
+            pl.loop(half * SOME, half * SOME + SOME)(lambda level: complete(turn, level))
             if turn == 0:
                 send_faces(1, half)
-
-    def inner(turn):
-        levels(turn, 1, take_edges(turn, 1), 0, LEV)
 
     def early(group):
         if group < 2:
@@ -423,11 +453,13 @@
             send_edges(0, 1)
 
     def rest():
+        alone(0, 0)
         outer(0)
         send_edges(1, 0)
-        inner(0)
+        alone(0, 1)
         send_edges(1, 1)
-        inner(1)
+        alone(1, 0)
+        alone(1, 1)
         outer(1)
         for copy in copies.values():
             copy.wait_send()
@@ -480,7 +512,11 @@
     recv,
     face_send,
     face_recv,
+    landed,
+    load_sem,
 ):
+    load = pltpu.make_async_copy(ensemble_ref, landed, load_sem)
+    load.start()
     at, beside = place()[-2:]
     peers = [at(0, 0, 0, 1)] + [at(0, d, 0, 0) for d in range(1, 4)]
     peers += [at(0, 0, d, 0) for d in range(1, 8)] + [at(d, 0, 0, 0) for d in range(1, 4)]
@@ -489,8 +525,13 @@
     for peer in peers:
         pl.semaphore_signal(barrier, inc=1, device_id=peer, device_id_type=MESH)
 
+    load.wait()
     for row in range(ROWS):
-        state[row] = ensemble_ref[pl.ds(row, M, stride=ROWS), :]
+        state[row] = landed[pl.ds(row, M, stride=ROWS), :]
+
+    def enter():
+        pl.semaphore_wait(barrier, len(peers))
+
     early, rest = transport(
         speed_x_ref, speed_y_ref, state, out_ref, middle, face, got, edge, came, face_send,
         face_recv,
@@ -500,22 +541,23 @@
             block, scale_ref, weight_ref, state, column_x_ref, column_y_ref, peak_ref, part,
             gathered,
         )
-        if block == 0:
-            pl.semaphore_wait(barrier, len(peers))
         whole = (whole_0, whole_1)[block]
         from_core = (from_core_0, from_core_1)[block]
         from_y = (from_y_0, from_y_1)[block]
         from_z = (from_z_0, from_z_1)[block]
         from_x = (from_x_0, from_x_1)[block]
-        share(
-            block, produce, owner_ref, part, whole, from_core, sums, from_y, from_z, from_x, send,
-            recv,
-        )
+
+        def share_now(meanwhile, digest):
+            return share(
+                block, enter if block == 0 else None, produce, meanwhile, digest, owner_ref, part, whole, from_core, sums, from_y,
+                from_z, from_x, send, recv,
+            )
+
         then = None if block < NBLK - 1 else early
         assimilate(
             block, owner_ref, error_ref, state, whole, observed_ref, column_x_ref, column_y_ref,
             peak_ref, spread, scaled, innovation, pert, solved_t, taper_y, taper_vx, system, weight,
-            then,
+            share_now, then,
         )
     rest()
 
@@ -540,7 +582,7 @@
     result = pl.pallas_call(
         filter_kernel,
         out_shape=jax.ShapeDtypeStruct((M * ROWS, CY), F32),
-        in_specs=[SMEM_SPEC] * 4 + [VMEM_SPEC] * 7,
+        in_specs=[SMEM_SPEC] * 4 + [pl.BlockSpec(memory_space=pl.ANY)] + [VMEM_SPEC] * 6,
         out_specs=VMEM_SPEC,
         scratch_shapes=[
             pltpu.VMEM((ROWS, M, CY), F32),
@@ -552,10 +594,10 @@
             *[pltpu.VMEM((3, 2 * M, 128), F32)] * NBLK,
             *[pltpu.VMEM((8, PIECE, 128), F32)] * NBLK,
             *[pltpu.VMEM((4, PIECE, 128), F32)] * NBLK,
-            pltpu.VMEM((M, NCH * NB), F32),
-            pltpu.VMEM((M + 8, NCH * NB), F32),
-            pltpu.VMEM((1, NCH * NB), F32),
-            pltpu.VMEM((M, NCH * NB), BF16),
+            pltpu.VMEM((NCH, M, NB), F32),
+            pltpu.VMEM((M + 8, NB), F32),
+            pltpu.VMEM((NCH, 1, NB), F32),
+            pltpu.VMEM((NCH, M, NB), BF16),
             pltpu.VMEM((NCH * NB, M), BF16),
             pltpu.VMEM((CY, NB), F32),
             pltpu.VMEM((ROWS, NB), F32),
@@ -570,6 +612,8 @@
             pltpu.SemaphoreType.DMA((NBLK, N_COPIES)),
             pltpu.SemaphoreType.DMA((N_FACES,)),
             pltpu.SemaphoreType.DMA((N_FACES,)),
+            pltpu.VMEM((M * ROWS, CY), F32),
+            pltpu.SemaphoreType.DMA,
         ],
         compiler_params=pltpu.CompilerParams(
             vmem_limit_bytes=VMEM_LIMIT, collective_id=0, has_side_effects=True

time: 130 us -> 130 us (level)
  no operation moved by 1% of the time
where the time goes in v4:
time: 130 us; the launch traced here: 129 us
  Pallas kernels  127 us (98%)
  local copies, waits for them, and re-layouts  2.67 us (2%)
    pallas_call x1, Pallas kernels, shards(): pl.pallas_call(filter_kernel, out_shape=jax.ShapeDtypeStruct((M * ROWS, C...  127 us
    unnamed x1, local copies, waits for them, and re-layouts  2.67 us

profile of v4, /device:TPU:32, one launch (start us, length us, event | category | flops | bytes accessed | tf_op | source)
XLA Modules:
  0.0 129.4 jit_solution(2672149847206100317)
XLA Ops:
  0.0 126.7 %filter.1 = f32[3072,128]{1,0:T(8,128)} custom-call(f32[8]{0:T(128)} %scale_ref.1, f32[4,8]{1,0:T(4,128)} %weight_ref.1, f32[4]{0:T(128)} %error_ref.1, s32[2]{0:T(128)} %owner_ref.1, f32[3072,128]{1,0:T(8,128)} %bitcast.5, f32[2,4,512]{2,1,0:T(4,128)} %observed_ref.1, s32[2,512]{1,0:T(2,128)} %column_x_ref.1, s32[2,512]{1,0:T(2,128)} %column_y_ref.1, ...), custom_call_target="tpu_custom_call" | custom-call | tf_op jit(solution)/shard_map/filter/pallas_call | solution.py:582
  126.7 2.7 %copy.13 = f32[96,8,4,128]{3,2,1,0:T(4,128)} copy(f32[96,8,4,128]{3,2,1,0:T(4,128)} %bitcast.4) | data formatting | bytes 3145728

commit v5 on v4

--- a/solution.py
+++ b/solution.py
@@ -383,7 +383,7 @@
                 packed = jnp.where(here, turned, packed)
             return packed
 
-        edge[turn, kind] = lax.fori_loop(0, LEV, pack, jnp.zeros((M, CY), F32))
+        edge[turn, kind] = lax.fori_loop(0, LEV, pack, jnp.zeros((M, CY), F32)).astype(BF16)
         for n in range(2):
             start(
                 ("y", turn, kind, n), edge.at[turn, kind], came.at[turn, kind, n], targets[2 + n]
@@ -394,8 +394,8 @@
             copies["y", turn, kind, n].wait_recv()
         return jnp.where(
             lax.rem(lane, 2) == 1,
-            came[turn, kind, 0],
-            pltpu.roll(came[turn, kind, 1], CY - 2, 1),
+            came[turn, kind, 0].astype(F32),
+            pltpu.roll(came[turn, kind, 1].astype(F32), CY - 2, 1),
         )
 
     def advance(turn, kind, edges, level):
@@ -606,8 +606,8 @@
             pltpu.VMEM((ROWS, M, CY), F32),
             pltpu.VMEM((2, 2, LEV, M, CY), BF16),
             pltpu.VMEM((2, 2, LEV, M, CY), BF16),
-            pltpu.VMEM((2, 2, M, CY), F32),
-            pltpu.VMEM((2, 2, 2, M, CY), F32),
+            pltpu.VMEM((2, 2, M, CY), BF16),
+            pltpu.VMEM((2, 2, 2, M, CY), BF16),
             pltpu.SemaphoreType.DMA((NBLK, N_COPIES)),
             pltpu.SemaphoreType.DMA((NBLK, N_COPIES)),
             pltpu.SemaphoreType.DMA((N_FACES,)),

time: 130 us -> 127 us (0.977)
  Pallas kernels: 127 us -> 124 us
    pallas_call x1, Pallas kernels: 127 us -> 124 us  [shards(): pl.pallas_call(filter_kernel, out_shape=jax.ShapeDtypeStruct((M * ROWS, C...]
where the time goes in v5:
time: 127 us; the launch traced here: 126 us
  Pallas kernels  124 us (98%)
  local copies, waits for them, and re-layouts  2.67 us (2%)
    pallas_call x1, Pallas kernels, shards(): pl.pallas_call(filter_kernel, out_shape=jax.ShapeDtypeStruct((M * ROWS, C...  124 us
    unnamed x1, local copies, waits for them, and re-layouts  2.67 us

profile of v5, /device:TPU:32, one launch (start us, length us, event | category | flops | bytes accessed | tf_op | source)
XLA Modules:
  0.0 126.2 jit_solution(16122217101763941206)
XLA Ops:
  0.0 123.6 %filter.1 = f32[3072,128]{1,0:T(8,128)} custom-call(f32[8]{0:T(128)} %scale_ref.1, f32[4,8]{1,0:T(4,128)} %weight_ref.1, f32[4]{0:T(128)} %error_ref.1, s32[2]{0:T(128)} %owner_ref.1, f32[3072,128]{1,0:T(8,128)} %bitcast.5, f32[2,4,512]{2,1,0:T(4,128)} %observed_ref.1, s32[2,512]{1,0:T(2,128)} %column_x_ref.1, s32[2,512]{1,0:T(2,128)} %column_y_ref.1, ...), custom_call_target="tpu_custom_call" | custom-call | tf_op jit(solution)/shard_map/filter/pallas_call | solution.py:582
  123.6 2.7 %copy.13 = f32[96,8,4,128]{3,2,1,0:T(4,128)} copy(f32[96,8,4,128]{3,2,1,0:T(4,128)} %bitcast.4) | data formatting | bytes 3145728
